TPU v7x, 128 devices: a whole 4x4x4 slice. The times are simulated.
128 devices in a mesh: ctx: 32 (over x, z_lo, y), chan: 4 (over z_hi, core).
Axes of the slice: x: 4, y: 4, z: 4 (z_hi: 2, z_lo: 2; z = z_hi * 2 + z_lo), core: 2. Of those that a mesh axis runs over, the one named last changes fastest.
Arguments:
- queries: bfloat16 [4096, 4096], P('ctx', 'chan'), may hold values from -8 to 8
- key_rows: bfloat16 [4096, 4096], P('ctx', 'chan'), may hold values from -8 to 8
- value_rows: bfloat16 [4096, 4096], P('ctx', 'chan'), may hold values from -16 to 16
- gate_in: bfloat16 [4096, 4096], P('ctx', 'chan'), may hold values from -6 to 6
- gate_out: bfloat16 [4096, 4096], P('ctx', 'chan'), may hold values from -6 to 6
- kernel_taps: float32 [512, 7], P('chan'), may hold values from -2 to 2
- norm_gain: float32 [4096], P('chan'), may hold values from 0.1 to 1.9
- cotangent: bfloat16 [4096, 4096], P('ctx', 'chan'), may hold values from -6 to 6
Outputs:
- mixed: bfloat16 [4096, 4096], P('ctx', 'chan')
- grad_queries: bfloat16 [4096, 4096], P('ctx', 'chan')
- grad_keys: bfloat16 [4096, 4096], P('ctx', 'chan')
- grad_values: bfloat16 [4096, 4096], P('ctx', 'chan')
- grad_gate_in: bfloat16 [4096, 4096], P('ctx', 'chan')
- grad_gate_out: bfloat16 [4096, 4096], P('ctx', 'chan')
- grad_filter: float32 [512, 7], P('chan')
- grad_gain: float32 [4096], P('chan')
All inputs are finite; a program needn't handle non-finite values.
Results may differ from a plain program's by a relative error of at most 0.015.
Values may be sent and summed in bfloat16 or wider, within the bound.
A program may use at most 128 MiB of HBM per device.

v0:
```python
import jax
import jax.numpy as jnp
from jax import lax
from jax.sharding import Mesh
from jax.sharding import PartitionSpec as P

HEAD = 128
FILT = 7
WIDTH = 4096
CTX = ("ctx_0", "ctx_1", "ctx_2")


EPS = 1e-06
NEG = -1e30


def laid_out(pieces, dim):
    lengths = list(pieces.shape[1:])
    lengths[dim] *= pieces.shape[0]
    return jnp.moveaxis(pieces, 0, dim).reshape(lengths)


def all_blocks(shard, axes, order):
    pieces = shard[None]
    for k in order:
        pieces = lax.all_gather(pieces, axes[k], axis=0, tiled=True)
    current = [lax.axis_size(axes[k]) for k in reversed(order)]
    pieces = pieces.reshape(*current, *shard.shape)
    turned = sorted(range(len(order)), key=lambda place: order[len(order) - 1 - place])
    return pieces.transpose(*turned, *range(len(order), pieces.ndim)).reshape(-1, *shard.shape)


def whole_of(shard, axes, order, dim):
    return laid_out(all_blocks(shard, axes, order), dim)


def sent_to_all(shard, axis):
    length = lax.axis_size(axis)
    return lax.all_to_all(
        jnp.broadcast_to(shard[None], (length, *shard.shape)), axis, 0, 0, tiled=True
    )


def taken_together(shard, axis):
    return sent_to_all(shard, axis).sum(axis=0)


def from_behind(shard, axis, by):
    length = lax.axis_size(axis)
    pairs = [(i, i + by) for i in range(length) if 0 <= i + by < length]
    return lax.ppermute(shard, axis, pairs)


def packed_total(arrays, axis):
    ends = [0]
    for a in arrays:
        ends.append(ends[-1] + a.size)
    subtotal = taken_together(jnp.concatenate([a.ravel() for a in arrays]), axis)
    return tuple((subtotal[b:e].reshape(a.shape) for a, b, e in zip(arrays, ends, ends[1:])))


def side_by_side(arrays, axis, dim, along):
    ends, at = ([], 0)
    for a in arrays[:-1]:
        at += a.shape[along]
        ends.append(at)
    both = jnp.concatenate(arrays, axis=along)
    return tuple(jnp.split(lax.all_gather(both, axis, axis=dim, tiled=True), ends, axis=along))


def score_block(query_heads, key_block, query_pos, key_pos):
    scores = jnp.einsum(
        "rhe,khe->hrk", query_heads, key_block, preferred_element_type=jnp.float32
    ) * HEAD ** (-0.5)
    allowed = query_pos[:, None] >= key_pos[None, :]
    return jnp.where(allowed[None], scores, NEG)


def row_totals(query_heads, query_pos, block_count, keys_heads, block_rows):
    row_count = query_heads.shape[0]
    head_count = query_heads.shape[1]

    def advance(block_index, running):
        row_max, row_sum = running
        first_key = block_index * block_rows
        key_block = lax.dynamic_slice_in_dim(keys_heads, first_key, block_rows, 0)
        key_pos = first_key + jnp.arange(block_rows, dtype=jnp.int32)
        scores = score_block(query_heads, key_block, query_pos, key_pos)
        new_max = jnp.maximum(row_max, jnp.max(scores, axis=2))
        row_sum = row_sum * jnp.exp(row_max - new_max) + jnp.sum(
            jnp.exp(scores - new_max[:, :, None]), axis=2
        )
        return (new_max, row_sum)

    initial = (
        jnp.full((head_count, row_count), NEG, jnp.float32),
        jnp.zeros((head_count, row_count), jnp.float32),
    )
    row_max, row_sum = lax.fori_loop(0, block_count, advance, initial)
    return row_max + jnp.log(row_sum)


def row_outputs(query_heads, query_pos, block_count, keys_heads, values_heads, lse, block_rows):
    row_count = query_heads.shape[0]
    head_count = query_heads.shape[1]

    def advance(block_index, summed):
        first_key = block_index * block_rows
        key_block = lax.dynamic_slice_in_dim(keys_heads, first_key, block_rows, 0)
        value_block = lax.dynamic_slice_in_dim(values_heads, first_key, block_rows, 0)
        key_pos = first_key + jnp.arange(block_rows, dtype=jnp.int32)
        scores = score_block(query_heads, key_block, query_pos, key_pos)
        weights_low = jnp.exp(scores - lse[:, :, None]).astype(jnp.bfloat16)
        return summed + jnp.einsum(
            "hrk,khe->rhe", weights_low, value_block, preferred_element_type=jnp.float32
        )

    summed = lax.fori_loop(
        0, block_count, advance, jnp.zeros((row_count, head_count, HEAD), jnp.float32)
    )
    return summed.reshape(row_count, head_count * HEAD).astype(jnp.bfloat16)


def query_grads(
    query_heads, d_heads, query_pos, block_count, keys_heads, values_heads, lse, delta, block_rows
):
    row_count = query_heads.shape[0]
    head_count = query_heads.shape[1]

    def advance(block_index, summed):
        first_key = block_index * block_rows
        key_block = lax.dynamic_slice_in_dim(keys_heads, first_key, block_rows, 0)
        value_block = lax.dynamic_slice_in_dim(values_heads, first_key, block_rows, 0)
        key_pos = first_key + jnp.arange(block_rows, dtype=jnp.int32)
        scores = score_block(query_heads, key_block, query_pos, key_pos)
        weights = jnp.exp(scores - lse[:, :, None])
        d_probs = jnp.einsum(
            "rhe,khe->hrk", d_heads, value_block, preferred_element_type=jnp.float32
        )
        d_scores = (weights * (d_probs - delta[:, :, None])).astype(jnp.bfloat16)
        return summed + jnp.einsum(
            "hrk,khe->rhe", d_scores, key_block, preferred_element_type=jnp.float32
        )

    summed = lax.fori_loop(
        0, block_count, advance, jnp.zeros((row_count, head_count, HEAD), jnp.float32)
    )
    return (summed * HEAD ** (-0.5)).reshape(row_count, head_count * HEAD).astype(jnp.bfloat16)


def shards(queries, key_rows, value_rows, gate_in, gate_out, kernel_taps, norm_gain, cotangent):
    row_count = queries.shape[0]
    channels = queries.shape[1]
    head_count = channels // HEAD
    group_count = kernel_taps.shape[0]
    devices = lax.axis_size(CTX)
    position = lax.axis_index(CTX)
    own_first = position * row_count
    total_rows = row_count * devices
    block_rows = min(512, total_rows)
    local_pos = jnp.arange(row_count, dtype=jnp.int32)
    keys_all, values_all = (
        whole_of(key_rows, CTX, (1, 0, 2), 0),
        whole_of(value_rows, CTX, (1, 0, 2), 0),
    )
    keys_heads = keys_all.reshape(total_rows, head_count, HEAD)
    query_sets = (queries, own_first + local_pos)
    query_block, query_pos = query_sets
    block_count = query_pos[-1] // block_rows + 1
    lse_sets = row_totals(
        query_block.reshape(-1, head_count, HEAD), query_pos, block_count, keys_heads, block_rows
    )
    values_heads = values_all.reshape(total_rows, head_count, HEAD)
    query_block, query_pos = query_sets
    outputs = row_outputs(
        query_block.reshape(-1, head_count, HEAD),
        query_pos,
        block_count,
        keys_heads,
        values_heads,
        lse_sets,
        block_rows,
    )
    lse_rows = lse_sets.T
    attn_wide = outputs.astype(jnp.float32)
    square_sum = taken_together(jnp.sum(attn_wide * attn_wide, axis=1), "chan")
    inverse_rms = 1.0 / jnp.sqrt(square_sum / WIDTH + EPS)
    normed = attn_wide * inverse_rms[:, None] * norm_gain[None, :]
    gate_wide = gate_in.astype(jnp.float32)
    mixed_in = gate_wide * normed
    taps = jnp.broadcast_to(
        kernel_taps[:, None, :], (group_count, channels // group_count, FILT)
    ).reshape(channels, FILT)
    rim_before = from_behind(mixed_in[row_count - (FILT - 1) :], CTX, 1)
    extended = jnp.concatenate([rim_before, mixed_in], axis=0)
    conv_out = jnp.zeros((row_count, channels), jnp.float32)
    for lag in range(FILT):
        conv_out = (
            conv_out + taps[:, lag][None, :] * extended[FILT - 1 - lag : FILT - 1 - lag + row_count]
        )
    out_gate = gate_out.astype(jnp.float32)
    mixed = (out_gate * conv_out).astype(jnp.bfloat16)
    upstream = cotangent.astype(jnp.float32)
    grad_gate_out = (upstream * conv_out).astype(jnp.bfloat16)
    d_conv = upstream * out_gate
    tap_columns = []
    for lag in range(FILT):
        per_channel = jnp.sum(
            d_conv * extended[FILT - 1 - lag : FILT - 1 - lag + row_count], axis=0
        )
        tap_columns.append(per_channel.reshape(group_count, -1).sum(axis=1))
    tap_terms = jnp.stack(tap_columns, axis=1)
    rim_after = from_behind(d_conv[: FILT - 1], CTX, -1)
    extended_grad = jnp.concatenate([d_conv, rim_after], axis=0)
    d_mixed = jnp.zeros((row_count, channels), jnp.float32)
    for lag in range(FILT):
        d_mixed = d_mixed + taps[:, lag][None, :] * extended_grad[lag : lag + row_count]
    grad_gate_in = (d_mixed * normed).astype(jnp.bfloat16)
    d_normed = d_mixed * gate_wide
    gain_terms = jnp.sum(d_normed * attn_wide * inverse_rms[:, None], axis=0)
    grad_filter, grad_gain = packed_total((tap_terms, gain_terms), CTX)
    scaled = d_normed * norm_gain[None, :]
    row_dot = taken_together(jnp.sum(scaled * attn_wide, axis=1), "chan")
    d_attn = (
        inverse_rms[:, None] * scaled - attn_wide * (inverse_rms**3 * row_dot / WIDTH)[:, None]
    ).astype(jnp.bfloat16)
    d_heads = d_attn.reshape(row_count, head_count, HEAD)
    delta_rows = jnp.sum(
        d_heads.astype(jnp.float32) * attn_wide.reshape(row_count, head_count, HEAD), axis=2
    )
    own_count = (own_first + row_count - 1) // block_rows + 1
    grad_queries = query_grads(
        queries.reshape(row_count, head_count, HEAD),
        d_heads,
        own_first + local_pos,
        own_count,
        keys_heads,
        values_heads,
        lse_rows.T,
        delta_rows.T,
        block_rows,
    )
    lse_all, delta_all = side_by_side((lse_rows, delta_rows), CTX, 0, 1)
    own_keys = key_rows.reshape(row_count, head_count, HEAD)
    own_values = value_rows.reshape(row_count, head_count, HEAD)
    key_pos = own_first + local_pos
    empty_grad = jnp.zeros((row_count, head_count, HEAD), jnp.float32)
    query_piece, d_piece = side_by_side((queries, d_attn), CTX, 0, 1)
    piece_rows = query_piece.shape[0]

    def contribute(totals):
        query_heads = query_piece.reshape(piece_rows, head_count, HEAD)
        piece_heads = d_piece.reshape(piece_rows, head_count, HEAD)
        query_pos = jnp.arange(piece_rows, dtype=jnp.int32)
        lse_piece = lse_all.T
        delta_piece = delta_all.T
        scores = score_block(query_heads, own_keys, query_pos, key_pos)
        weights = jnp.exp(scores - lse_piece[:, :, None])
        d_probs = jnp.einsum(
            "rhe,khe->hrk", piece_heads, own_values, preferred_element_type=jnp.float32
        )
        d_scores = (weights * (d_probs - delta_piece[:, :, None])).astype(jnp.bfloat16)
        key_grad = jnp.einsum(
            "hrk,rhe->khe", d_scores, query_heads, preferred_element_type=jnp.float32
        )
        value_grad = jnp.einsum(
            "hrk,rhe->khe",
            weights.astype(jnp.bfloat16),
            piece_heads,
            preferred_element_type=jnp.float32,
        )
        return (key_grad, value_grad)

    def unchanged(totals):
        return totals

    key_grad, value_grad = lax.cond(
        jnp.int32(0) + piece_rows > own_first, contribute, unchanged, (empty_grad, empty_grad)
    )
    grad_keys = (key_grad * HEAD ** (-0.5)).reshape(row_count, channels).astype(jnp.bfloat16)
    grad_values = value_grad.reshape(row_count, channels).astype(jnp.bfloat16)
    return (
        mixed,
        grad_queries,
        grad_keys,
        grad_values,
        grad_gate_in,
        grad_gate_out,
        grad_filter,
        grad_gain,
    )


def solution(mesh):
    torus = Mesh(
        mesh.devices.reshape(4, 2, 4, mesh.shape["chan"]), ("ctx_0", "ctx_1", "ctx_2", "chan")
    )
    in_specs = (
        P(CTX, "chan"),
        P(CTX, "chan"),
        P(CTX, "chan"),
        P(CTX, "chan"),
        P(CTX, "chan"),
        P("chan", None),
        P("chan"),
        P(CTX, "chan"),
    )
    out_specs = (
        P(CTX, "chan"),
        P(CTX, "chan"),
        P(CTX, "chan"),
        P(CTX, "chan"),
        P(CTX, "chan"),
        P(CTX, "chan"),
        P("chan", None),
        P("chan"),
    )
    return jax.shard_map(
        shards, mesh=torus, in_specs=in_specs, out_specs=out_specs, check_vma=False
    )
```

profile of v0, /device:TPU:0, one launch (start us, length us, event | category | flops | bytes accessed | tf_op | source)
XLA Modules:
  0.0 607.9 jit_solution(2018437885724615930)
XLA Ops:
  7.2 10.9 %all-gather.1 = bf16[256,1024]{1,0:T(8,128)(2,1)} all-gather(bf16[128,1024]{1,0:T(8,128)(2,1)} %param.17), channel_id=3, replica_groups=mesh['ctx_0'=4,'ctx_1'=2,'ctx_2'=4,'chan'=4] {'ctx_1'}, dimensions={0}, use_global_device_ids=true | all-gather | bytes 786432 | tf_op jit(solution)/shard_map/all_gather | solution.py:26
  18.2 8.5 %all-gather = bf16[256,1024]{1,0:T(8,128)(2,1)} all-gather(bf16[128,1024]{1,0:T(8,128)(2,1)} %param.18), channel_id=2, replica_groups=mesh['ctx_0'=4,'ctx_1'=2,'ctx_2'=4,'chan'=4] {'ctx_1'}, dimensions={0}, use_global_device_ids=true | all-gather | bytes 786432 | tf_op jit(solution)/shard_map/all_gather | solution.py:26
  26.8 24.3 %all-gather.12.cloned.1.call-done = bf16[8,128,1024]{2,1,0:T(8,128)(2,1)} async-done(((bf16[2,128,1024]{2,1,0:T(8,128)(2,1)}), bf16[8,128,1024]{2,1,0:T(8,128)(2,1)}) %all-gather.12.cloned.1.call-update) | async-done | bytes 2097168 | tf_op jit(solution)/shard_map/all_gather | solution.py:26
  51.2 32.5 %all-gather.8.cloned.1.call-done = bf16[8,128,1024]{2,1,0:T(8,128)(2,1)} async-done(((bf16[2,128,1024]{2,1,0:T(8,128)(2,1)}), bf16[8,128,1024]{2,1,0:T(8,128)(2,1)}) %all-gather.8.cloned.1.call-update) | async-done | bytes 2097168 | tf_op jit(solution)/shard_map/all_gather | solution.py:26
  83.6 1.1 convert_multiply_fusion.1
  84.8 1.3 collective-permute-start.1
  89.3 1.1 copy.172
  91.0 77.5 %all-gather.14.cloned.1.call-done = bf16[32,128,1024]{2,1,0:T(8,128)(2,1)} async-done(((bf16[8,128,1024]{2,1,0:T(8,128)(2,1)}), bf16[32,128,1024]{2,1,0:T(8,128)(2,1)}) %all-gather.14.cloned.1.call-update) | async-done | bytes 8388624 | tf_op jit(solution)/shard_map/all_gather | solution.py:26
  168.5 8.2 %copy.171 = bf16[4,2,4,128,1024]{4,3,2,1,0:T(8,128)(2,1)} copy(bf16[4,2,4,128,1024]{4,3,1,0,2:T(8,128)(2,1)} %bitcast.176) | data formatting | bytes 16777216 | tf_op jit(solution)/shard_map/transpose | solution.py:30
  176.7 9.3 %copy.217 = bf16[512,8,8,128]{3,2,1,0:T(8,128)(2,1)} copy(bf16[512,8,8,128]{3,1,2,0:T(8,128)(2,1)} %bitcast.172) | data formatting | bytes 16777216
  186.0 7.8 %copy.176 = bf16[4096,8,128]{2,0,1:T(8,128)(2,1)} copy(bf16[4096,8,128]{2,1,0:T(8,128)(2,1)} %bitcast.173) | data formatting | bytes 16777216
  193.8 2.4 while.35
  194.0 1.7 fusion.135
  196.2 57.9 %all-gather.10.cloned.1.call-done = bf16[32,128,1024]{2,1,0:T(8,128)(2,1)} async-done(((bf16[8,128,1024]{2,1,0:T(8,128)(2,1)}), bf16[32,128,1024]{2,1,0:T(8,128)(2,1)}) %all-gather.10.cloned.1.call-update) | async-done | bytes 8388624 | tf_op jit(solution)/shard_map/all_gather | solution.py:26
  254.2 8.2 %copy.170 = bf16[4,2,4,128,1024]{4,3,2,1,0:T(8,128)(2,1)} copy(bf16[4,2,4,128,1024]{4,3,1,0,2:T(8,128)(2,1)} %bitcast.175) | data formatting | bytes 16777216 | tf_op jit(solution)/shard_map/transpose | solution.py:30
  262.3 8.8 %copy.216 = bf16[512,8,8,128]{3,2,1,0:T(8,128)(2,1)} copy(bf16[512,8,8,128]{3,1,2,0:T(8,128)(2,1)} %bitcast.174) | data formatting | bytes 16777216
  271.2 3.9 while.36
  271.4 1.3 constant_dynamic-slice_fusion.4
  272.7 2.4 fusion.139
  275.8 4.4 all-to-all-start
  280.4 4.9 all-to-all-done
  285.4 1.2 multiply_convert_fusion.1
  286.9 7.6 %all_to_all.18 = f32[4,1,128]{2,1,0:T(1,128)S(1)} all-to-all(f32[4,1,128]{2,1,0:T(1,128)S(1)} %broadcast_in_dim.106), channel_id=1, replica_groups=mesh['ctx_0'=4,'ctx_1'=2,'ctx_2'=4,'chan'=4] {'chan'}, dimensions={0} | all-to-all | bytes 4096 | tf_op jit(solution)/shard_map/all_to_all | solution.py:39
  294.8 0.9 pad_maximum_fusion.2
  296.3 3.3 collective-permute-start
  300.8 0.8 broadcast.153
  301.6 6.5 %while.37 = (s32[]{:T(128)}, f32[128,8,128]{0,2,1:T(8,128)}, s32[]{:T(128)}, bf16[4096,8,128]{2,0,1:T(8,128)(2,1)}, bf16[128,8,128]{2,0,1:T(8,128)(2,1)S(1)}, /*...) while((s32[]{:T(128)}, f32[128,8,128]{0,2,1:T(8,128)}, ...), condition=%wide.region_12.13_spmd.clone, body=%wide.region_11.12_spmd.clone.sunk | while | flops 405996160 | bytes 11154631 | solution.py:145
  301.8 1.3 constant_dynamic-slice_fusion.5
  303.1 1.7 fusion.145
  304.8 3.4 fusion.146
  308.1 1.1 multiply_convert_fusion.3
  309.2 0.9 copy.202
  310.1 4.0 fusion.71
  314.1 4.2 multiply_reduce_fusion.1
  320.1 0.8 broadcast_in_dim.107
  320.9 78.4 %all-to-all-start.2 = ((f32[32,1,1920]{2,1,0:T(1,128)}), f32[32,1,1920]{2,1,0:T(1,128)S(1)}, u32[]{:S(2)}, u32[]{:S(2)}) async-start(f32[32,1,1920]{2,1,0:T(1,128)} %broadcast_in_dim.107), calls=%async_computation.2 | async-start | bytes 491520 | tf_op jit(solution)/shard_map/all_to_all | solution.py:39
  399.4 84.7 %all_gather.31 = f32[4096,16]{0,1:T(8,128)S(1)} all-gather(f32[128,16]{0,1:T(8,128)S(1)} %pad_maximum_fusion.3), channel_id=1, replica_groups=mesh['ctx_0'=4,'ctx_1'=2,'ctx_2'=4,'chan'=4] {'ctx_0','ctx_1','ctx_2'}, dimensions={0}, use_global_device_ids=true | all-gather | bytes 270336 | tf_op jit(solution)/shard_map/all_gather | solution.py:68
  484.1 30.8 %all-to-all-done.2 = f32[32,1,1920]{2,1,0:T(1,128)S(1)} async-done(((f32[32,1,1920]{2,1,0:T(1,128)}), f32[32,1,1920]{2,1,0:T(1,128)S(1)}, u32[]{:S(2)}, u32[]{:S(2)}) %all-to-all-start.2) | async-done | bytes 245792 | tf_op jit(solution)/shard_map/all_to_all | solution.py:39
  516.5 1.2 all-gather.16.cloned.1.call-done
  517.7 82.7 %conditional.1 = (f32[128,8,128]{0,2,1:T(8,128)S(1)}, bf16[128,1024]{1,0:T(8,128)(2,1)}) conditional(s32[]{:T(128)} %convert_element_type.91, () %tuple.33, (s32[128]{0:T(128)S(1)}, bf16[4096,2048]{1,0:T(8,128)(2,1)}, bf16[128,1024]{1,0:T(8,128)(2,1)}, f32[4096,16]{0,1:T(8,128)S(1)}, bf16[128,1024]{1,0:T(8,128)(2,1)}) %tuple.34), branch_computations={%region_13.14_spmd, %region_14.15_spmd} | conditional | flops 4337565696 | bytes 269091584 | solution.py:277
  518.7 20.7 %copy.187 = bf16[4096,2048]{0,1:T(8,128)(2,1)} copy(bf16[4096,2048]{1,0:T(8,128)(2,1)} %get-tuple-element.471) | data formatting | bytes 33554432 | tf_op jit(solution)/shard_map
  539.4 11.7 %fusion.97 = (bf16[4096,1024]{0,1:T(8,128)(2,1)}, bf16[4096,1024]{0,1:T(8,128)(2,1)}) fusion(bf16[4096,2048]{0,1:T(8,128)(2,1)} %copy.187), kind=kLoop, calls=%fused_computation.153 | loop fusion | bytes 33554432 | tf_op jit(solution)/shard_map/split | solution.py:68
  551.2 11.9 %fusion.22 = f32[8,4096,128]{2,1,0:T(8,128)} fusion(bf16[4096,8,128]{0,2,1:T(8,128)(2,1)} %bitcast.169, bf16[128,1024]{1,0:T(8,128)(2,1)S(1)} %copy-done.2), kind=kOutput, calls=%fused_computation.17 | convolution fusion | flops 1073741824 | bytes 25427968 | tf_op jit(solution)/shard_map/cond/branch_1_fun/rhe,khe->hrk/dot_general | solution.py:72
  563.1 14.0 %fusion.15 = bf16[8,128,128]{1,2,0:T(8,128)(2,1)} fusion(bf16[4096,8,128]{0,2,1:T(8,128)(2,1)} %bitcast.177, f32[8,4096,128]{2,1,0:T(8,128)} %fusion.22, f32[8,4096]{1,0:T(8,128)S(1)} %get-tuple-element.550, pred[4096,128]{1,0:T(8,128)(4,1)S(1)} %iota_compare_fusion), kind=kOutput, calls=%fused_computation.14 | convolution fusion | flops 1090650112 | bytes 26083328 | tf_op jit(solution)/shard_map/cond/branch_1_fun/hrk,rhe->khe/dot_general | solution.py:266
  577.4 13.5 %multiply_convert_fusion.clone.6 = bf16[8,4096,128]{2,1,0:T(8,128)(2,1)} fusion(f32[8,4096,128]{2,1,0:T(8,128)S(1)} %copy-done, bf16[4096,8,128]{0,2,1:T(8,128)(2,1)S(1)} %bitcast.180, f32[8,4096]{1,0:T(8,128)S(1)} %copy-done.7, f32[8,4096]{1,0:T(8,128)S(1)} %get-tuple-element.550, ...), kind=kOutput, calls=%fused_computation.3.clone.clone.clone.clone.clone.1 | convolution fusion | flops 1098907648 | bytes 34603008 | tf_op jit(solution)/shard_map/cond/branch_1_fun/rhe,khe->hrk/dot_general | solution.py:259
  590.9 8.4 %fusion.14 = f32[128,8,128]{2,0,1:T(8,128)S(1)} fusion(bf16[4096,8,128]{0,2,1:T(8,128)(2,1)} %bitcast.170, bf16[8,4096,128]{2,1,0:T(8,128)(2,1)} %multiply_convert_fusion.clone.6), kind=kOutput, calls=%fused_computation.13 | convolution fusion | flops 1073741824 | bytes 17301504 | tf_op jit(solution)/shard_map/cond/branch_1_fun/hrk,rhe->khe/dot_general | solution.py:263
  599.6 0.9 copy.207
  600.5 0.9 copy.203
  (104 shorter events, 10.5 us)
Async XLA Ops:
  7.2 83.4 %copy-start.9 = (f32[128,7]{0,1:T(8,128)S(1)}, f32[128,7]{0,1:T(8,128)}, u32[]{:S(2)}) copy-start(f32[128,7]{0,1:T(8,128)} %param.21) | copy-start | bytes 10756
  7.2 43.9 %all-gather.12.cloned.1.call-start = ((), (), s32[]{:S(2)}) async-start(), calls=%async_computation.5 | async-start | bytes 2621440 | tf_op jit(solution)/shard_map/all_gather | solution.py:26
  18.2 65.4 %all-gather.8.cloned.1.call-start = ((), (), s32[]{:S(2)}) async-start(), calls=%async_computation.3 | async-start | bytes 2621440 | tf_op jit(solution)/shard_map/all_gather | solution.py:26
  26.8 141.8 %all-gather.14.cloned.1.call-start = ((), (), s32[]{:S(2)}) async-start(), calls=%async_computation.6 | async-start | bytes 10485760 | tf_op jit(solution)/shard_map/all_gather | solution.py:26
  51.1 203.0 %all-gather.10.cloned.1.call-start = ((), (), s32[]{:S(2)}) async-start(), calls=%async_computation.4 | async-start | bytes 10485760 | tf_op jit(solution)/shard_map/all_gather | solution.py:26
  84.8 200.7 %collective-permute-start.1 = (f32[6,1024]{1,0:T(8,128)S(1)}, f32[6,1024]{1,0:T(8,128)S(1)}, u32[]{:S(2)}, u32[]{:S(2)}) collective-permute-start(f32[6,1024]{1,0:T(8,128)S(1)} %slice.127), channel_id=1, source_target_pairs={{4,0},{8,4},{12,8},{16,12},{20,16},{24,20},{28,24},{32,28},{36,32}... | collective-permute-start | bytes 73736 | tf_op jit(solution)/shard_map/ppermute | solution.py:51
  271.1 14.3 %copy-start.8 = (f32[1024]{0:T(1024)S(1)}, f32[1024]{0:T(1024)}, u32[]{:S(2)}) copy-start(f32[1024]{0:T(1024)} %param.22) | copy-start | bytes 12292
  271.1 15.5 %copy-start.4 = (bf16[128,1024]{1,0:T(8,128)(2,1)S(1)}, bf16[128,1024]{1,0:T(8,128)(2,1)}, u32[]{:S(2)}) copy-start(bf16[128,1024]{1,0:T(8,128)(2,1)} %param.19) | copy-start | bytes 786436
  271.2 23.6 %copy-start.3 = (bf16[128,1024]{1,0:T(8,128)(2,1)S(1)}, bf16[128,1024]{1,0:T(8,128)(2,1)}, u32[]{:S(2)}) copy-start(bf16[128,1024]{1,0:T(8,128)(2,1)} %param.16) | copy-start | bytes 786436
  275.8 9.6 %all-to-all-start = ((f32[4,1,128]{2,1,0:T(1,128)}), f32[4,1,128]{2,1,0:T(1,128)S(1)}, u32[]{:S(2)}, u32[]{:S(2)}) async-start(f32[4,1,128]{2,1,0:T(1,128)} %broadcast_in_dim.105), calls=%async_computation | async-start | bytes 4096 | tf_op jit(solution)/shard_map/all_to_all | solution.py:39
  280.2 237.5 %all-gather.16.cloned.1.call-start = ((), (), s32[]{:S(2)}) async-start(), calls=%async_computation.7 | async-start | bytes 17301504 | tf_op jit(solution)/shard_map/all_gather | solution.py:68
  294.7 6.9 %copy-start.1 = (f32[128,1024]{1,0:T(8,128)}, f32[128,1024]{1,0:T(8,128)S(1)}, u32[]{:S(2)}) copy-start(f32[128,1024]{1,0:T(8,128)S(1)} %get-tuple-element.555) | copy-start | bytes 1572868
  296.3 13.8 %collective-permute-start = (f32[6,1024]{1,0:T(8,128)}, f32[6,1024]{1,0:T(8,128)S(1)}, u32[]{:S(2)}, u32[]{:S(2)}) collective-permute-start(f32[6,1024]{1,0:T(8,128)} %slice.111), channel_id=1, source_target_pairs={{0,4},{4,8},{8,12},{12,16},{16,20},{20,24},{24,28},{28,32},{32,36}... | collective-permute-start | bytes 73736 | tf_op jit(solution)/shard_map/ppermute | solution.py:51
  320.9 194.0 %all-to-all-start.2 = ((f32[32,1,1920]{2,1,0:T(1,128)}), f32[32,1,1920]{2,1,0:T(1,128)S(1)}, u32[]{:S(2)}, u32[]{:S(2)}) async-start(f32[32,1,1920]{2,1,0:T(1,128)} %broadcast_in_dim.107), calls=%async_computation.2 | async-start | bytes 491520 | tf_op jit(solution)/shard_map/all_to_all | solution.py:39
  539.4 11.7 %copy-start.2 = (bf16[128,1024]{1,0:T(8,128)(2,1)S(1)}, bf16[128,1024]{1,0:T(8,128)(2,1)}, u32[]{:S(2)}) copy-start(bf16[128,1024]{1,0:T(8,128)(2,1)} %get-tuple-element.152) | copy-start | bytes 786436 | tf_op jit(solution)/shard_map/cond
  551.2 25.9 %slice-start = ((s8[8388608]{0:T(1024)(128)(4,1)}), s8[4194304]{0:T(1024)(128)(4,1)S(1)}, s32[]{:S(2)}) async-start(s8[8388608]{0:T(1024)(128)(4,1)} %bitcast.178), calls=%async_computation.8 | async-start | bytes 8388608 | tf_op jit(solution)/shard_map/cond
  563.1 14.0 %copy-start = (f32[8,4096,128]{2,1,0:T(8,128)S(1)}, f32[8,4096,128]{2,1,0:T(8,128)}, u32[]{:S(2)}) copy-start(f32[8,4096,128]{2,1,0:T(8,128)} %fusion.22) | copy-start | bytes 50331652 | tf_op jit(solution)/shard_map/cond
  563.1 14.3 %slice-start.1 = ((s8[8388608]{0:T(1024)(128)(4,1)}), s8[4194304]{0:T(1024)(128)(4,1)S(1)}, s32[]{:S(2)}) async-start(s8[8388608]{0:T(1024)(128)(4,1)} %bitcast.178), calls=%async_computation.9 | async-start | bytes 8388608 | tf_op jit(solution)/shard_map/cond
  563.1 14.3 %copy-start.5 = (bf16[128,1024]{1,0:T(8,128)(2,1)S(1)}, bf16[128,1024]{1,0:T(8,128)(2,1)}, u32[]{:S(2)}) copy-start(bf16[128,1024]{1,0:T(8,128)(2,1)} %get-tuple-element.154) | copy-start | bytes 786436 | tf_op jit(solution)/shard_map/cond
  563.1 14.3 %copy-start.7 = (f32[8,4096]{1,0:T(8,128)S(1)}, f32[8,4096]{1,0:T(8,128)}, u32[]{:S(2)}) copy-start(f32[8,4096]{1,0:T(8,128)} %get-tuple-element.551) | copy-start | bytes 393220 | tf_op jit(solution)/shard_map/cond
  590.9 8.6 %copy-start.6 = (bf16[8,128,128]{1,2,0:T(8,128)(2,1)S(1)}, bf16[8,128,128]{1,2,0:T(8,128)(2,1)}, u32[]{:S(2)}) copy-start(bf16[8,128,128]{1,2,0:T(8,128)(2,1)} %fusion.15) | copy-start | bytes 786436 | tf_op jit(solution)/shard_map/cond
Sparse Core Ops, SparseCore 0:
  18.3 32.7 all-gather.11
  52.7 30.8 all-gather.7
  85.3 83.1 all-gather.13
  170.0 84.0 all-gather.9
  295.8 221.8 all-gather.15
where the time goes:
time: 611 us; the launch traced here: 608 us
  waiting for transfers between devices  229 us (37%)
  blocking collectives  112 us (18%)
  local copies, waits for them, and re-layouts  89.9 us (15%)
  starting transfers between devices  87.7 us (14%)
  matrix products  57 us (9%)
  between operations  16.7 us (3%)
  other arithmetic  15.5 us (3%)
    all_gather x4, waiting for transfers between devices, all_blocks(): pieces = lax.all_gather(pieces, axes[k], axis=0, tiled=True)  192 us
    all_gather x1, blocking collectives, side_by_side(): lax.all_gather(both, axis, axis=dim, tiled=True)  84.7 us
    all_to_all x2, starting transfers between devices, sent_to_all(): lax.all_to_all(jnp.broadcast_to(shard[None], (length, *shard.shape)), axi...  82.9 us
    all_to_all x2, waiting for transfers between devices, sent_to_all(): lax.all_to_all(jnp.broadcast_to(shard[None], (length, *shard.shape)), axi...  35.8 us
    unnamed x18, local copies, waits for them, and re-layouts  28.7 us
    another operation x3, local copies, waits for them, and re-layouts  21.6 us
    all_gather x2, blocking collectives, all_blocks(): pieces = lax.all_gather(pieces, axes[k], axis=0, tiled=True)  19.4 us
    transpose x2, local copies, waits for them, and re-layouts, all_blocks(): pieces.transpose(*turned, *range(len(order), pieces.ndim))  16.4 us
  transfers between devices with their start and end apart: 9, of which 7 were waited for; matrix products, arithmetic and copies ran while one was open for 13% of the time, Pallas kernels for 0%

commit v1 on v0

v1 whole, which is shorter than its diff:
```python
import functools
import math

import jax
import jax.numpy as jnp
from jax import lax
from jax.experimental import pallas as pl
from jax.experimental.pallas import tpu as pltpu
from jax.sharding import PartitionSpec as P

HEAD = 128
FILT = 7
WIDTH = 4096
EPS = 1e-06
NEG = -1e30
SCALE = HEAD ** (-0.5)
SCALE2 = SCALE * math.log2(math.e)
BLOCK = 128
CHUNK = 512
F32 = jnp.float32
BF16 = jnp.bfloat16


def dot(a, b, ca, cb, precision=None):
    return lax.dot_general(
        a, b, (((ca,), (cb,)), ((), ())), preferred_element_type=F32, precision=precision
    )


def kernel(
    q_ref, k_ref, v_ref, gi_ref, go_ref, taps_ref, gain_ref, cot_ref,
    mixed_ref, gq_ref, gk_ref, gv_ref, ggi_ref, ggo_ref, gf_ref, gg_ref,
    kvs, qs, ssrc, kvb, qb, sb, du, dz, ot, lse2, osrc, ob, stat_in, tot, hst,
    dqs, dqb, dk_acc, dv_acc, dkvs, dkvb, zx, gsrc, gin,
    kv_send, q_send, s_send, o_send, st_send, h_send, dq_send, dkv_send, g_send, rim_send,
    kv_recv, q_recv, s_recv, o_recv, st_recv, h_recv, dq_recv, dkv_recv, g_recv, rim_recv,
):
    p = lax.axis_index("ctx")
    chan = lax.axis_index("chan")
    zh, core = chan // 2, chan % 2
    x, z, y = p // 8, (p // 4) % 2, p % 4
    host = x * 4 + y
    hl0, m0 = host // 2, host % 2
    home_chan = zh * 2 + z
    r0 = m0 * 2 + core
    head0 = home_chan * 8 + hl0

    def chip(bit, e):
        return (e // 4) * 8 + bit * 4 + e % 4

    def send(src, dst, send_sem, recv_sem, p2, chan2):
        own = jnp.logical_and(p2 == p, chan2 == chan)

        @pl.when(own)
        def _():
            pltpu.make_async_copy(src, dst, recv_sem).start()

        @pl.when(jnp.logical_not(own))
        def _():
            pltpu.make_async_remote_copy(
                src_ref=src, dst_ref=dst, send_sem=send_sem, recv_sem=recv_sem,
                device_id={"ctx": p2, "chan": chan2}, device_id_type=pl.DeviceIdType.MESH,
            ).start()

    def sent(src, dst, send_sem, recv_sem, p2, chan2):
        own = jnp.logical_and(p2 == p, chan2 == chan)

        @pl.when(jnp.logical_not(own))
        def _():
            pltpu.make_async_remote_copy(
                src_ref=src, dst_ref=dst, send_sem=send_sem, recv_sem=recv_sem,
                device_id={"ctx": p2, "chan": chan2}, device_id_type=pl.DeviceIdType.MESH,
            ).wait_send()

    def arrived(buf, recv_sem):
        pltpu.make_async_copy(buf, buf, recv_sem).wait()

    def kv_plan(i):
        e, c2 = (host + i // 2) % 16, (core + i) % 2
        return kvs.at[e // 2], kvb.at[p], kv_send.at[i], kv_recv, chip(core, e), zh * 2 + c2

    own_chunk = p // 4
    own_r = jnp.minimum(own_chunk, 7 - own_chunk)
    own_slot = (own_chunk // 4) * 4 + p % 4

    def q_plan(i):
        hl = (hl0 + i) % 8
        return (
            qs.at[hl], qb.at[own_slot], q_send.at[i], q_recv,
            chip(core, hl * 2 + own_r // 2), zh * 2 + own_r % 2,
        )

    def s_plan(i):
        hl = (hl0 + i) % 8
        return (
            ssrc.at[hl], sb.at[own_slot], s_send.at[i], s_recv,
            chip(core, hl * 2 + own_r // 2), zh * 2 + own_r % 2,
        )

    def slot_home(slot):
        return jnp.where(slot < 4, r0 * 4 + slot, (7 - r0) * 4 + slot - 4)

    def o_plan(i):
        return osrc.at[i], ob.at[hl0], o_send.at[i], o_recv, slot_home(i), home_chan

    def dq_plan(i):
        return dqs.at[i], dqb.at[hl0], dq_send.at[i], dq_recv, slot_home(i), home_chan

    def dkv_plan(i):
        p2 = (p + i) % 32
        return dkvs.at[p2], dkvb.at[r0 * 8 + hl0], dkv_send.at[i], dkv_recv, p2, home_chan

    def st_plan(i):
        g = (head0 + i) % 32
        return (
            stat_in.at[head0], stat_in.at[head0], st_send.at[i], st_recv,
            chip((g // 8) % 2, (g % 8) * 2 + m0), (g // 16) * 2 + core,
        )

    def g_plan(i):
        return gsrc, gin.at[p], g_send.at[i], g_recv, (p + i) % 32, chan

    def each(plan, count, act, first=0):
        lax.fori_loop(first, count, lambda i, _: (act(*plan(i)), 0)[1], 0)

    du[pl.ds(0, BLOCK), :] = cot_ref[...].astype(F32) * go_ref[...].astype(F32)

    def rim_copy(src, dst, j, p2):
        return pltpu.make_async_remote_copy(
            src_ref=src, dst_ref=dst, send_sem=rim_send.at[j], recv_sem=rim_recv.at[j],
            device_id={"ctx": p2, "chan": chan}, device_id_type=pl.DeviceIdType.MESH,
        )

    du_rim = rim_copy(du.at[pl.ds(0, 8)], du.at[pl.ds(BLOCK, 8)], 0, jnp.maximum(p - 1, 0))
    z_rim = rim_copy(zx.at[pl.ds(BLOCK, 8)], zx.at[pl.ds(0, 8)], 1, jnp.minimum(p + 1, 31))

    @pl.when(p > 0)
    def _():
        du_rim.start()

    for hl in range(8):
        cols = slice(hl * HEAD, (hl + 1) * HEAD)
        kvs[hl, 0] = k_ref[:, cols]
        kvs[hl, 1] = v_ref[:, cols]
        qs[hl] = q_ref[:, cols]
    each(kv_plan, 32, send)
    each(q_plan, 8, send)

    group_of = lax.broadcasted_iota(jnp.int32, (128, 1024), 1) // 8
    spread = (group_of == lax.broadcasted_iota(jnp.int32, (128, 1024), 0)).astype(F32)
    taps = dot(taps_ref[...], spread, 0, 0, lax.Precision.HIGHEST)
    gain = gain_ref[...]

    @pl.when(p == 31)
    def _():
        du[pl.ds(BLOCK, 8), :] = jnp.zeros((8, 1024), F32)

    @pl.when(p < 31)
    def _():
        du_rim.wait_recv()

    for hl in range(8):
        cols = slice(hl * HEAD, (hl + 1) * HEAD)
        total = taps[0:1, cols] * du[pl.ds(0, BLOCK), cols]
        for lag in range(1, FILT):
            total = total + taps[lag : lag + 1, cols] * du[pl.ds(lag, BLOCK), cols]
        dz[:, cols] = total
        ssrc[hl] = (total * gi_ref[:, cols].astype(F32) * gain[:, cols]).astype(BF16)
    each(s_plan, 8, send)

    arrived(kvb, kv_recv)
    arrived(qb, q_recv)
    below = lax.broadcasted_iota(jnp.int32, (CHUNK, CHUNK), 0) <= lax.broadcasted_iota(
        jnp.int32, (CHUNK, CHUNK), 1
    )

    def keys_of(kt):
        return kvb[pl.ds(kt * 4, 4), 0].reshape(CHUNK, HEAD)

    def values_of(kt):
        return kvb[pl.ds(kt * 4, 4), 1].reshape(CHUNK, HEAD)

    s_waited = False
    for qc in range(2):
        chunk = r0 if qc == 0 else 7 - r0
        rows = slice(qc * CHUNK, (qc + 1) * CHUNK)
        q_rows = qb[pl.ds(qc * 4, 4)].reshape(CHUNK, HEAD)

        def forward(kt, carry, masked, q_rows=q_rows):
            top, norm, acc = carry
            s = dot(keys_of(kt), q_rows, 1, 1)
            if masked:
                s = jnp.where(below, s, NEG)
            new_top = jnp.maximum(top, jnp.max(s, axis=0, keepdims=True))
            w = jnp.exp2(s * SCALE2 - new_top * SCALE2)
            fade = jnp.exp2((top - new_top) * SCALE2)
            norm = norm * fade + jnp.sum(w, axis=0, keepdims=True)
            acc = acc * fade + dot(values_of(kt), w.astype(BF16), 0, 0)
            return new_top, norm, acc

        carry = (
            jnp.full((1, CHUNK), NEG, F32), jnp.zeros((1, CHUNK), F32), jnp.zeros((HEAD, CHUNK), F32)
        )
        carry = lax.fori_loop(0, chunk, lambda kt, c: forward(kt, c, False), carry)
        top, norm, acc = forward(chunk, carry, True)
        out = (acc * (1.0 / norm)).astype(BF16)
        out_wide = out.astype(F32)
        ot[:, rows] = out_wide
        lse2[:, rows] = top * SCALE2 + jnp.log2(norm)
        osrc[pl.ds(qc * 4, 4)] = out_wide.T.astype(BF16).reshape(4, HEAD, HEAD)
        if not s_waited:
            arrived(sb, s_recv)
            s_waited = True
        s_t = sb[pl.ds(qc * 4, 4)].reshape(CHUNK, HEAD).astype(F32).T
        squares = jnp.sum(out_wide * out_wide, axis=0, keepdims=True)
        dots = jnp.sum(s_t * out_wide, axis=0, keepdims=True)
        for j in range(4):
            at = slice(j * HEAD, (j + 1) * HEAD)
            stat_in[head0, 0, qc * 4 + j : qc * 4 + j + 1, :] = squares[:, at]
            stat_in[head0, 1, qc * 4 + j : qc * 4 + j + 1, :] = dots[:, at]

    each(st_plan, 32, send, 1)
    each(o_plan, 8, send)
    arrived(stat_in.at[pl.ds(0, 31)], st_recv)
    tot[...] = jnp.sum(stat_in[...], axis=0)

    home_slot = jnp.where(r0 % 2 == hl0 // 4, hl0 % 4, 4 + hl0 % 4)
    h_args = (tot, hst, h_send, h_recv, slot_home(home_slot), home_chan)
    send(*h_args)

    rstd_all = lax.rsqrt(tot[0] / WIDTH + EPS)
    drop_all = rstd_all * rstd_all * rstd_all * tot[1] / WIDTH

    def clear(kt, _):
        dk_acc[pl.ds(kt * CHUNK, CHUNK), :] = jnp.zeros((CHUNK, HEAD), F32)
        dv_acc[pl.ds(kt * CHUNK, CHUNK), :] = jnp.zeros((CHUNK, HEAD), F32)
        return 0

    lax.fori_loop(0, 8, clear, 0)
    for qc in range(2):
        chunk = r0 if qc == 0 else 7 - r0
        rows = slice(qc * CHUNK, (qc + 1) * CHUNK)
        q_rows = qb[pl.ds(qc * 4, 4)].reshape(CHUNK, HEAD)
        s_t = sb[pl.ds(qc * 4, 4)].reshape(CHUNK, HEAD).astype(F32).T
        lanes = lambda a: jnp.concatenate([a[qc * 4 + j : qc * 4 + j + 1] for j in range(4)], axis=1)
        out_wide = ot[:, rows]
        d_out_t = (lanes(rstd_all) * s_t - out_wide * lanes(drop_all)).astype(BF16)
        d_wide = d_out_t.astype(F32)
        delta = jnp.sum(d_wide * out_wide, axis=0, keepdims=True)
        d_rows = d_wide.T.astype(BF16)
        lse_row = lse2[:, rows]

        def backward(kt, dq_t, masked, q_rows=q_rows, d_out_t=d_out_t, d_rows=d_rows, delta=delta,
                     lse_row=lse_row):
            k_rows = keys_of(kt)
            s = dot(k_rows, q_rows, 1, 1)
            if masked:
                s = jnp.where(below, s, NEG)
            w = jnp.exp2(s * SCALE2 - lse_row)
            d_w = dot(values_of(kt), d_out_t, 1, 0)
            d_s = (w * (d_w - delta)).astype(BF16)
            at = pl.ds(pl.multiple_of(kt * CHUNK, CHUNK), CHUNK)
            dk_acc[at, :] += dot(d_s, q_rows, 1, 0)
            dv_acc[at, :] += dot(w.astype(BF16), d_rows, 1, 0)
            return dq_t + dot(k_rows, d_s, 0, 0)

        dq_t = jnp.zeros((HEAD, CHUNK), F32)
        dq_t = lax.fori_loop(0, chunk, lambda kt, c: backward(kt, c, False), dq_t)
        dq_t = backward(chunk, dq_t, True)
        dqs[pl.ds(qc * 4, 4)] = (dq_t * SCALE).T.astype(BF16).reshape(4, HEAD, HEAD)

    def to_low(kt, _):
        at = pl.ds(pl.multiple_of(kt * CHUNK, CHUNK), CHUNK)
        dkvs[pl.ds(kt * 4, 4), 0] = (dk_acc[at, :] * SCALE).astype(BF16).reshape(4, HEAD, HEAD)
        dkvs[pl.ds(kt * 4, 4), 1] = dv_acc[at, :].astype(BF16).reshape(4, HEAD, HEAD)
        return 0

    lax.fori_loop(0, 8, to_low, 0)
    each(dkv_plan, 32, send)
    each(dq_plan, 8, send)

    arrived(ob, o_recv)
    arrived(hst, h_recv)
    square_row = hst[0, pl.ds(own_slot, 1), :]
    rstd_row = lax.rsqrt(square_row / WIDTH + EPS)
    rstd = jnp.broadcast_to(rstd_row, (BLOCK, BLOCK)).T
    for hl in range(8):
        cols = slice(hl * HEAD, (hl + 1) * HEAD)
        a_hat = ob[hl].astype(F32) * rstd
        normed = a_hat * gain[:, cols]
        gate = gi_ref[:, cols].astype(F32)
        zx[pl.ds(8, BLOCK), cols] = gate * normed
        ggi_ref[:, cols] = (dz[:, cols] * normed).astype(BF16)
        gsrc[1, hl : hl + 1, :] = jnp.sum(dz[:, cols] * gate * a_hat, axis=0, keepdims=True)

    @pl.when(p < 31)
    def _():
        z_rim.start()

    @pl.when(p == 0)
    def _():
        zx[pl.ds(0, 8), :] = jnp.zeros((8, 1024), F32)

    @pl.when(p > 0)
    def _():
        z_rim.wait_recv()

    tap_sums = []
    for hl in range(8):
        cols = slice(hl * HEAD, (hl + 1) * HEAD)
        d_conv = du[pl.ds(0, BLOCK), cols]
        conv = jnp.zeros((BLOCK, HEAD), F32)
        sums = []
        for lag in range(FILT):
            shifted = zx[pl.ds(8 - lag, BLOCK), cols]
            conv = conv + taps[lag : lag + 1, cols] * shifted
            sums.append(jnp.sum(d_conv * shifted, axis=0, keepdims=True))
        sums.append(jnp.zeros((1, HEAD), F32))
        tap_sums.append(jnp.concatenate(sums, axis=0))
        mixed_ref[:, cols] = (go_ref[:, cols].astype(F32) * conv).astype(BF16)
        ggo_ref[:, cols] = (cot_ref[:, cols].astype(F32) * conv).astype(BF16)
    gsrc[0] = dot(jnp.concatenate(tap_sums, axis=1), spread, 1, 1, lax.Precision.HIGHEST)
    each(g_plan, 32, send, 1)

    arrived(gin.at[pl.ds(0, 31)], g_recv)
    gin[p] = gsrc[...]
    g_total = jnp.sum(gin[...], axis=0)
    gf_ref[...] = g_total[0]
    gg_ref[...] = g_total[1]
    arrived(dqb, dq_recv)
    arrived(dkvb, dkv_recv)
    for hl in range(8):
        cols = slice(hl * HEAD, (hl + 1) * HEAD)
        gq_ref[:, cols] = dqb[hl]
        for which, out_ref in ((0, gk_ref), (1, gv_ref)):
            total = dkvb[hl, which].astype(F32)
            for r in range(1, 4):
                total = total + dkvb[r * 8 + hl, which].astype(F32)
            out_ref[:, cols] = total.astype(BF16)

    each(kv_plan, 32, sent)
    each(q_plan, 8, sent)
    each(s_plan, 8, sent)
    each(st_plan, 32, sent, 1)
    each(o_plan, 8, sent)
    sent(*h_args)
    each(dkv_plan, 32, sent)
    each(dq_plan, 8, sent)
    each(g_plan, 32, sent, 1)

    @pl.when(p > 0)
    def _():
        du_rim.wait_send()

    @pl.when(p < 31)
    def _():
        z_rim.wait_send()


def shards(queries, key_rows, value_rows, gate_in, gate_out, kernel_taps, norm_gain, cotangent):
    rows = jax.ShapeDtypeStruct((BLOCK, 1024), BF16)
    vmem = pl.BlockSpec(memory_space=pltpu.VMEM)
    tile = (HEAD, HEAD)
    dma = pltpu.SemaphoreType.DMA
    outs = pl.pallas_call(
        kernel,
        out_shape=[rows] * 6 + [jax.ShapeDtypeStruct((8, 128), F32)] * 2,
        in_specs=[vmem] * 8,
        out_specs=[vmem] * 8,
        scratch_shapes=[
            pltpu.VMEM((8, 2, *tile), BF16),
            pltpu.VMEM((8, *tile), BF16),
            pltpu.VMEM((8, *tile), BF16),
            pltpu.VMEM((32, 2, *tile), BF16),
            pltpu.VMEM((8, *tile), BF16),
            pltpu.VMEM((8, *tile), BF16),
            pltpu.VMEM((BLOCK + 8, 1024), F32),
            pltpu.VMEM((BLOCK, 1024), F32),
            pltpu.VMEM((HEAD, 1024), F32),
            pltpu.VMEM((1, 1024), F32),
            pltpu.VMEM((8, *tile), BF16),
            pltpu.VMEM((8, *tile), BF16),
            pltpu.VMEM((32, 2, 8, 128), F32),
            pltpu.VMEM((2, 8, 128), F32),
            pltpu.VMEM((2, 8, 128), F32),
            pltpu.VMEM((8, *tile), BF16),
            pltpu.VMEM((8, *tile), BF16),
            pltpu.VMEM((4096, HEAD), F32),
            pltpu.VMEM((4096, HEAD), F32),
            pltpu.VMEM((32, 2, *tile), BF16),
            pltpu.VMEM((32, 2, *tile), BF16),
            pltpu.VMEM((BLOCK + 8, 1024), F32),
            pltpu.VMEM((2, 8, 128), F32),
            pltpu.VMEM((32, 2, 8, 128), F32),
            dma((32,)), dma((8,)), dma((8,)), dma((8,)), dma((32,)), dma, dma((8,)), dma((32,)), dma((32,)),
            dma((2,)),
            dma, dma, dma, dma, dma, dma, dma, dma, dma, dma((2,)),
        ],
        compiler_params=pltpu.CompilerParams(has_side_effects=True, vmem_limit_bytes=56 * 1024 * 1024),
        name="hyena",
    )(
        queries, key_rows, value_rows, gate_in, gate_out, kernel_taps, norm_gain.reshape(1, -1), cotangent
    )
    mixed, gq, gk, gv, ggi, ggo, gf, gg = outs
    return mixed, gq, gk, gv, ggi, ggo, gf[:FILT].T, gg.reshape(-1)


def solution(mesh):
    wide = P("ctx", "chan")
    thin = (P("chan", None), P("chan"))
    return jax.shard_map(
        shards, mesh=mesh, in_specs=(wide,) * 5 + thin + (wide,), out_specs=(wide,) * 6 + thin, check_vma=False
    )
```

time: 611 us -> 139 us (0.23)
  waiting for transfers between devices: 229 us -> 0 us
  Pallas kernels: 0 us -> 128 us
  blocking collectives: 112 us -> 0 us
  starting transfers between devices: 87.7 us -> 0 us
  local copies, waits for them, and re-layouts: 89.9 us -> 9.88 us
  matrix products: 57 us -> 0 us
  between operations: 16.7 us -> 0.66 us
  other arithmetic: 15.5 us -> 0 us
    all_gather x5 -> x0, waiting for transfers between devices: 193 us -> none  [the longest x4 192 us: all_blocks(): pieces = lax.all_gather(pieces, axes[k], axis=0, tiled=True)]
    pallas_call x0 -> x1, Pallas kernels: none -> 128 us  [shards(): pl.pallas_call(kernel, out_shape=[rows] * 6 + [jax.ShapeDtypeStruct((8, 1...]
    all_gather x3 -> x0, blocking collectives: 104 us -> none  [the longest x1 84.7 us: side_by_side(): lax.all_gather(both, axis, axis=dim, tiled=True)]
    all_to_all x2 -> x0, starting transfers between devices: 82.9 us -> none  [sent_to_all(): lax.all_to_all(jnp.broadcast_to(shard[None], (length, *shard.shape)), axi...]
    dot_general x8 -> x0, matrix products: 57 us -> none  [the longest x3 15.3 us: score_block(): jnp.einsum('rhe,khe->hrk', query_heads, key_block, preferred_element_type...]
    all_to_all x2 -> x0, waiting for transfers between devices: 35.8 us -> none  [sent_to_all(): lax.all_to_all(jnp.broadcast_to(shard[None], (length, *shard.shape)), axi...]
    another operation x5 -> x0, local copies, waits for them, and re-layouts: 21.7 us -> none
    unnamed x18 -> x22, local copies, waits for them, and re-layouts: 28.7 us -> 9.28 us
  transfers between devices with their start and end apart: 9 -> 0, of which waited for: 7 -> 0; matrix products, arithmetic and copies ran while one was open for 13% -> 0% of each run, Pallas kernels for 0% -> 0%
where the time goes in v1:
time: 139 us
  Pallas kernels  128 us (92%)
  local copies, waits for them, and re-layouts  9.88 us (7%)
    pallas_call x1, Pallas kernels, shards(): pl.pallas_call(kernel, out_shape=[rows] * 6 + [jax.ShapeDtypeStruct((8, 1...  128 us
    unnamed x22, local copies, waits for them, and re-layouts  9.28 us

profile of v1, /device:TPU:0, one launch (start us, length us, event | category | flops | bytes accessed | tf_op | source)
XLA Modules:
  0.0 138.5 jit_solution(16492725664731123956)
XLA Ops:
  0.6 1.4 %copy.16.taps_ref = f32[128,7]{1,0:T(8,128)} copy(f32[128,7]{0,1:T(8,128)} %param.13) | data formatting | bytes 7168 | tf_op args[5]
  2.1 128.0 %hyena.1 = (bf16[128,1024]{1,0:T(8,128)(2,1)}, bf16[128,1024]{1,0:T(8,128)(2,1)}, bf16[128,1024]{1,0:T(8,128)(2,1)}, bf16[128,1024]{1,0:T(8,128)(2,1)}, bf16[128...) custom-call(bf16[128,1024]{1,0:T(8,128)(2,1)} %q_ref.1, ...), custom_call_target="tpu_custom_call" | custom-call | tf_op jit(solution)/shard_map/hyena/pallas_call | solution.py:365
  130.0 0.0 copy-start.6
  130.1 0.7 copy-done.6
  130.7 0.6 slice_bitcast_fusion
  131.3 0.0 copy-start.4
  131.3 1.7 %copy.24 = bf16[128,1024]{1,0:T(8,128)(2,1)} copy(bf16[128,1024]{1,0:T(8,128)(2,1)} %get-tuple-element.32) | data formatting | bytes 524288
  133.0 0.0 copy-done.4
  133.0 0.0 copy-start.3
  133.0 0.7 copy.25
  133.7 0.3 copy-done.3
  134.1 0.0 copy-start.2
  134.1 0.7 copy.26
  134.8 0.3 copy-done.2
  135.1 0.0 copy-start.1
  135.1 0.7 copy.27
  135.8 0.3 copy-done.1
  136.2 0.0 copy-start
  136.2 0.7 copy.28
  136.9 0.3 copy-done
  137.2 0.0 copy-start.5
  137.2 0.7 copy.29
  137.9 0.0 copy-done.5
  137.9 0.6 copy.30
Async XLA Ops:
  130.0 0.7 copy-start.6
  131.3 1.7 %copy-start.4 = (bf16[128,1024]{1,0:T(8,128)(2,1)S(1)}, bf16[128,1024]{1,0:T(8,128)(2,1)}, u32[]{:S(2)}) copy-start(bf16[128,1024]{1,0:T(8,128)(2,1)} %get-tuple-element.33) | copy-start | bytes 786436
  133.0 1.0 copy-start.3
  134.1 1.0 copy-start.2
  135.1 1.0 copy-start.1
  136.2 1.0 copy-start
  137.2 0.7 copy-start.5

commit v2 on v1

--- a/solution.py
+++ b/solution.py
@@ -28,10 +28,11 @@
 
 
 def kernel(
-    q_ref, k_ref, v_ref, gi_ref, go_ref, taps_ref, gain_ref, cot_ref,
+    q_any, k_any, v_any, gi_any, go_any, taps_ref, gain_ref, cot_any,
     mixed_ref, gq_ref, gk_ref, gv_ref, ggi_ref, ggo_ref, gf_ref, gg_ref,
     kvs, qs, ssrc, kvb, qb, sb, du, dz, ot, lse2, osrc, ob, stat_in, tot, hst,
-    dqs, dqb, dk_acc, dv_acc, dkvs, dkvb, zx, gsrc, gin,
+    dqs, dqb, dq_acc, d_out_t, d_rows, delta, kv_acc, sibs, sibb, dkvs, dkvb, zx, gsrc, gin,
+    gi_ref, go_ref, cot_ref, wbuf, tops, in_sem, relay_send, relay_recv, sib_send, sib_recv,
     kv_send, q_send, s_send, o_send, st_send, h_send, dq_send, dkv_send, g_send, rim_send,
     kv_recv, q_recv, s_recv, o_recv, st_recv, h_recv, dq_recv, dkv_recv, g_recv, rim_recv,
 ):
@@ -76,8 +77,23 @@
         pltpu.make_async_copy(buf, buf, recv_sem).wait()
 
     def kv_plan(i):
-        e, c2 = (host + i // 2) % 16, (core + i) % 2
-        return kvs.at[e // 2], kvb.at[p], kv_send.at[i], kv_recv, chip(core, e), zh * 2 + c2
+        e = (host + i) % 16
+        return (
+            kvs.at[e // 2], kvb.at[p], kv_send.at[i], kv_recv.at[p // 2],
+            chip(core, e), zh * 2 + p % 2,
+        )
+
+    def relay_plan(i):
+        e = (host - 2 * (i // 2) - (host + core) % 2 + 16) % 16
+        source = chip(i % 2, e)
+        return (
+            kvb.at[source], kvb.at[source], relay_send.at[i], relay_recv,
+            p, zh * 2 + 1 - core, kv_recv.at[source // 2],
+        )
+
+    def relay(block, dst, send_sem, recv_sem, p2, chan2, landed):
+        arrived(block, landed)
+        send(block, dst, send_sem, recv_sem, p2, chan2)
 
     own_chunk = p // 4
     own_r = jnp.minimum(own_chunk, 7 - own_chunk)
@@ -106,9 +122,29 @@
     def dq_plan(i):
         return dqs.at[i], dqb.at[hl0], dq_send.at[i], dq_recv, slot_home(i), home_chan
 
+    last_chunk = 7 - 2 * m0
+
     def dkv_plan(i):
-        p2 = (p + i) % 32
-        return dkvs.at[p2], dkvb.at[r0 * 8 + hl0], dkv_send.at[i], dkv_recv, p2, home_chan
+        return (
+            dkvs.at[i // 4, i % 4], dkvb.at[m0 * 8 + hl0], dkv_send.at[i], dkv_recv,
+            ((i // 4) * 2 + core) * 4 + i % 4, home_chan,
+        )
+
+    def sib_copy(i):
+        return pltpu.make_async_remote_copy(
+            src_ref=sibs.at[i], dst_ref=sibb.at[i], send_sem=sib_send.at[i], recv_sem=sib_recv.at[i],
+            device_id={"ctx": p, "chan": zh * 2 + 1 - core}, device_id_type=pl.DeviceIdType.MESH,
+        )
+
+    def sib_sent(i):
+        @pl.when(i * 2 + 1 - core <= 7 - r0)
+        def _():
+            sib_copy(i).wait_send()
+
+    def dkv_sent(i):
+        @pl.when((i // 4) * 2 + core <= last_chunk)
+        def _():
+            sent(*dkv_plan(i))
 
     def st_plan(i):
         g = (head0 + i) % 32
@@ -123,6 +159,37 @@
     def each(plan, count, act, first=0):
         lax.fori_loop(first, count, lambda i, _: (act(*plan(i)), 0)[1], 0)
 
+    barrier = pltpu.get_barrier_semaphore()
+
+    def greet(i, _):
+        pl.semaphore_signal(
+            barrier, inc=1, device_id={"ctx": (p + i // 2) % 32, "chan": zh * 2 + (core + i) % 2},
+            device_id_type=pl.DeviceIdType.MESH,
+        )
+        return 0
+
+    def greet_far(i, _):
+        pl.semaphore_signal(
+            barrier, inc=1, device_id={"ctx": i * 2 + m0, "chan": (1 - zh) * 2 + core},
+            device_id_type=pl.DeviceIdType.MESH,
+        )
+        return 0
+
+    lax.fori_loop(1, 64, greet, 0)
+    lax.fori_loop(0, 16, greet_far, 0)
+    wide_in = [
+        pltpu.make_async_copy(src, dst, in_sem.at[j])
+        for j, (src, dst) in enumerate(((cot_any, cot_ref), (go_any, go_ref), (gi_any, gi_ref)))
+    ]
+    for copy in wide_in:
+        copy.start()
+    for hl in range(8):
+        cols = slice(hl * HEAD, (hl + 1) * HEAD)
+        pltpu.make_async_copy(k_any.at[:, cols], kvs.at[hl, 0], in_sem.at[3]).start()
+        pltpu.make_async_copy(v_any.at[:, cols], kvs.at[hl, 1], in_sem.at[3]).start()
+        pltpu.make_async_copy(q_any.at[:, cols], qs.at[hl], in_sem.at[4]).start()
+    wide_in[0].wait()
+    wide_in[1].wait()
     du[pl.ds(0, BLOCK), :] = cot_ref[...].astype(F32) * go_ref[...].astype(F32)
 
     def rim_copy(src, dst, j, p2):
@@ -134,22 +201,22 @@
     du_rim = rim_copy(du.at[pl.ds(0, 8)], du.at[pl.ds(BLOCK, 8)], 0, jnp.maximum(p - 1, 0))
     z_rim = rim_copy(zx.at[pl.ds(BLOCK, 8)], zx.at[pl.ds(0, 8)], 1, jnp.minimum(p + 1, 31))
 
-    @pl.when(p > 0)
-    def _():
-        du_rim.start()
-
-    for hl in range(8):
-        cols = slice(hl * HEAD, (hl + 1) * HEAD)
-        kvs[hl, 0] = k_ref[:, cols]
-        kvs[hl, 1] = v_ref[:, cols]
-        qs[hl] = q_ref[:, cols]
-    each(kv_plan, 32, send)
-    each(q_plan, 8, send)
-
     group_of = lax.broadcasted_iota(jnp.int32, (128, 1024), 1) // 8
     spread = (group_of == lax.broadcasted_iota(jnp.int32, (128, 1024), 0)).astype(F32)
-    taps = dot(taps_ref[...], spread, 0, 0, lax.Precision.HIGHEST)
+    taps = dot(taps_ref[...], spread, 1, 0, lax.Precision.HIGHEST)
     gain = gain_ref[...]
+
+    pltpu.make_async_copy(kvs, kvs, in_sem.at[3]).wait()
+    pltpu.make_async_copy(qs, qs, in_sem.at[4]).wait()
+    wide_in[2].wait()
+    pl.semaphore_wait(barrier, 79)
+
+    @pl.when(p > 0)
+    def _():
+        du_rim.start()
+
+    each(kv_plan, 16, send)
+    each(q_plan, 8, send)
 
     @pl.when(p == 31)
     def _():
@@ -166,9 +233,10 @@
             total = total + taps[lag : lag + 1, cols] * du[pl.ds(lag, BLOCK), cols]
         dz[:, cols] = total
         ssrc[hl] = (total * gi_ref[:, cols].astype(F32) * gain[:, cols]).astype(BF16)
+
+    each(relay_plan, 16, relay)
     each(s_plan, 8, send)
-
-    arrived(kvb, kv_recv)
+    arrived(kvb.at[pl.ds(0, 16)], relay_recv)
     arrived(qb, q_recv)
     below = lax.broadcasted_iota(jnp.int32, (CHUNK, CHUNK), 0) <= lax.broadcasted_iota(
         jnp.int32, (CHUNK, CHUNK), 1
@@ -186,16 +254,19 @@
         rows = slice(qc * CHUNK, (qc + 1) * CHUNK)
         q_rows = qb[pl.ds(qc * 4, 4)].reshape(CHUNK, HEAD)
 
-        def forward(kt, carry, masked, q_rows=q_rows):
+        def forward(kt, carry, masked, q_rows=q_rows, qc=qc):
             top, norm, acc = carry
             s = dot(keys_of(kt), q_rows, 1, 1)
             if masked:
                 s = jnp.where(below, s, NEG)
             new_top = jnp.maximum(top, jnp.max(s, axis=0, keepdims=True))
             w = jnp.exp2(s * SCALE2 - new_top * SCALE2)
+            w_low = w.astype(BF16)
+            wbuf[qc * 8 + kt] = w_low
+            tops[qc * 8 + kt] = new_top
             fade = jnp.exp2((top - new_top) * SCALE2)
             norm = norm * fade + jnp.sum(w, axis=0, keepdims=True)
-            acc = acc * fade + dot(values_of(kt), w.astype(BF16), 0, 0)
+            acc = acc * fade + dot(values_of(kt), w_low, 0, 0)
             return new_top, norm, acc
 
         carry = (
@@ -231,52 +302,78 @@
     rstd_all = lax.rsqrt(tot[0] / WIDTH + EPS)
     drop_all = rstd_all * rstd_all * rstd_all * tot[1] / WIDTH
 
-    def clear(kt, _):
-        dk_acc[pl.ds(kt * CHUNK, CHUNK), :] = jnp.zeros((CHUNK, HEAD), F32)
-        dv_acc[pl.ds(kt * CHUNK, CHUNK), :] = jnp.zeros((CHUNK, HEAD), F32)
-        return 0
-
-    lax.fori_loop(0, 8, clear, 0)
     for qc in range(2):
-        chunk = r0 if qc == 0 else 7 - r0
+        rows = slice(qc * CHUNK, (qc + 1) * CHUNK)
+        s_t = sb[pl.ds(qc * 4, 4)].reshape(CHUNK, HEAD).astype(F32).T
+        out_wide = ot[:, rows]
+
+        def lanes(a, qc=qc):
+            return jnp.concatenate([a[qc * 4 + j : qc * 4 + j + 1] for j in range(4)], axis=1)
+
+        d_low = (lanes(rstd_all) * s_t - out_wide * lanes(drop_all)).astype(BF16)
+        d_wide = d_low.astype(F32)
+        delta[:, rows] = jnp.sum(d_wide * out_wide, axis=0, keepdims=True)
+        d_out_t[:, rows] = d_low
+        d_rows[rows, :] = d_wide.T.astype(BF16)
+        dq_acc[:, rows] = jnp.zeros((HEAD, CHUNK), F32)
+
+    def backward(qc, kt, slot):
         rows = slice(qc * CHUNK, (qc + 1) * CHUNK)
         q_rows = qb[pl.ds(qc * 4, 4)].reshape(CHUNK, HEAD)
-        s_t = sb[pl.ds(qc * 4, 4)].reshape(CHUNK, HEAD).astype(F32).T
-        lanes = lambda a: jnp.concatenate([a[qc * 4 + j : qc * 4 + j + 1] for j in range(4)], axis=1)
-        out_wide = ot[:, rows]
-        d_out_t = (lanes(rstd_all) * s_t - out_wide * lanes(drop_all)).astype(BF16)
-        d_wide = d_out_t.astype(F32)
-        delta = jnp.sum(d_wide * out_wide, axis=0, keepdims=True)
-        d_rows = d_wide.T.astype(BF16)
-        lse_row = lse2[:, rows]
-
-        def backward(kt, dq_t, masked, q_rows=q_rows, d_out_t=d_out_t, d_rows=d_rows, delta=delta,
-                     lse_row=lse_row):
-            k_rows = keys_of(kt)
-            s = dot(k_rows, q_rows, 1, 1)
-            if masked:
-                s = jnp.where(below, s, NEG)
-            w = jnp.exp2(s * SCALE2 - lse_row)
-            d_w = dot(values_of(kt), d_out_t, 1, 0)
-            d_s = (w * (d_w - delta)).astype(BF16)
-            at = pl.ds(pl.multiple_of(kt * CHUNK, CHUNK), CHUNK)
-            dk_acc[at, :] += dot(d_s, q_rows, 1, 0)
-            dv_acc[at, :] += dot(w.astype(BF16), d_rows, 1, 0)
-            return dq_t + dot(k_rows, d_s, 0, 0)
-
-        dq_t = jnp.zeros((HEAD, CHUNK), F32)
-        dq_t = lax.fori_loop(0, chunk, lambda kt, c: backward(kt, c, False), dq_t)
-        dq_t = backward(chunk, dq_t, True)
-        dqs[pl.ds(qc * 4, 4)] = (dq_t * SCALE).T.astype(BF16).reshape(4, HEAD, HEAD)
-
-    def to_low(kt, _):
-        at = pl.ds(pl.multiple_of(kt * CHUNK, CHUNK), CHUNK)
-        dkvs[pl.ds(kt * 4, 4), 0] = (dk_acc[at, :] * SCALE).astype(BF16).reshape(4, HEAD, HEAD)
-        dkvs[pl.ds(kt * 4, 4), 1] = dv_acc[at, :].astype(BF16).reshape(4, HEAD, HEAD)
+        k_rows = keys_of(kt)
+        w = wbuf[qc * 8 + kt].astype(F32) * jnp.exp2(tops[qc * 8 + kt] * SCALE2 - lse2[:, rows])
+        d_w = dot(values_of(kt), d_out_t[:, rows], 1, 0)
+        d_s = (w * (d_w - delta[:, rows])).astype(BF16)
+        d_k = dot(d_s, q_rows, 1, 0)
+        d_v = dot(w.astype(BF16), d_rows[rows, :], 1, 0)
+        dq_acc[:, rows] += dot(k_rows, d_s, 0, 0)
+        if qc == 1:
+            kv_acc[slot, 0] = d_k
+            kv_acc[slot, 1] = d_v
+        else:
+            kv_acc[slot, 0] += d_k
+            kv_acc[slot, 1] += d_v
+
+    def finish(kt, slot):
+        @pl.when(jnp.logical_and(kt % 2 == core, kt <= last_chunk))
+        def _():
+            sib_copy(kt // 2).wait_recv()
+            for which, scale in ((0, SCALE), (1, 1.0)):
+                both = kv_acc[slot, which] * scale + sibb[kt // 2, which].astype(F32)
+                dkvs[kt // 2, :, which] = both.astype(BF16).reshape(4, HEAD, HEAD)
+            for j in range(4):
+                send(*dkv_plan((kt // 2) * 4 + j))
+
+    def key_chunk(t, _):
+        kt, slot = (hl0 + t) % 8, t % 2
+        for qc in (1, 0):
+            chunk = r0 if qc == 0 else 7 - r0
+
+            @pl.when(kt <= chunk)
+            def _():
+                backward(qc, kt, slot)
+
+        @pl.when(jnp.logical_and(kt % 2 != core, kt <= 7 - r0))
+        def _():
+            for which, scale in ((0, SCALE), (1, 1.0)):
+                sibs[kt // 2, which] = (kv_acc[slot, which] * scale).astype(BF16)
+            sib_copy(kt // 2).start()
+
+        @pl.when(jnp.logical_and(kt % 2 == core, kt > 7 - r0))
+        def _():
+            kv_acc[slot] = jnp.zeros((2, CHUNK, HEAD), F32)
+
+        @pl.when(t > 0)
+        def _():
+            finish((kt + 7) % 8, 1 - slot)
+
         return 0
 
-    lax.fori_loop(0, 8, to_low, 0)
-    each(dkv_plan, 32, send)
+    lax.fori_loop(0, 8, key_chunk, 0)
+    finish((hl0 + 7) % 8, 1)
+    for qc in range(2):
+        dq = dq_acc[:, qc * CHUNK : (qc + 1) * CHUNK] * SCALE
+        dqs[pl.ds(qc * 4, 4)] = dq.T.astype(BF16).reshape(4, HEAD, HEAD)
     each(dq_plan, 8, send)
 
     arrived(ob, o_recv)
@@ -325,26 +422,40 @@
     arrived(gin.at[pl.ds(0, 31)], g_recv)
     gin[p] = gsrc[...]
     g_total = jnp.sum(gin[...], axis=0)
-    gf_ref[...] = g_total[0]
+    gf_ref[...] = g_total[0, :FILT]
     gg_ref[...] = g_total[1]
     arrived(dqb, dq_recv)
-    arrived(dkvb, dkv_recv)
+
+    def all_keys(parts):
+        arrived(dkvb.at[pl.ds(0, parts * 8)], dkv_recv)
+        for hl in range(8):
+            cols = slice(hl * HEAD, (hl + 1) * HEAD)
+            for which, out_ref in ((0, gk_ref), (1, gv_ref)):
+                total = dkvb[hl, which]
+                if parts == 2:
+                    total = (total.astype(F32) + dkvb[8 + hl, which].astype(F32)).astype(BF16)
+                out_ref[:, cols] = total
+
     for hl in range(8):
-        cols = slice(hl * HEAD, (hl + 1) * HEAD)
-        gq_ref[:, cols] = dqb[hl]
-        for which, out_ref in ((0, gk_ref), (1, gv_ref)):
-            total = dkvb[hl, which].astype(F32)
-            for r in range(1, 4):
-                total = total + dkvb[r * 8 + hl, which].astype(F32)
-            out_ref[:, cols] = total.astype(BF16)
-
-    each(kv_plan, 32, sent)
+        gq_ref[:, hl * HEAD : (hl + 1) * HEAD] = dqb[hl]
+
+    @pl.when(own_chunk <= 5)
+    def _():
+        all_keys(2)
+
+    @pl.when(own_chunk > 5)
+    def _():
+        all_keys(1)
+
+    each(kv_plan, 16, sent)
+    each(relay_plan, 16, lambda *a: sent(*a[:6]))
+    lax.fori_loop(0, 4, lambda i, _: (sib_sent(i), 0)[1], 0)
     each(q_plan, 8, sent)
     each(s_plan, 8, sent)
     each(st_plan, 32, sent, 1)
     each(o_plan, 8, sent)
     sent(*h_args)
-    each(dkv_plan, 32, sent)
+    lax.fori_loop(0, 16, lambda i, _: (dkv_sent(i), 0)[1], 0)
     each(dq_plan, 8, sent)
     each(g_plan, 32, sent, 1)
 
@@ -355,17 +466,27 @@
     @pl.when(p < 31)
     def _():
         z_rim.wait_send()
+
+
+def handed_on(*refs):
+    sems = refs[16]
+    copies = [pltpu.make_async_copy(refs[i], refs[8 + i], sems.at[i]) for i in range(8)]
+    for copy in copies:
+        copy.start()
+    for copy in copies:
+        copy.wait()
 
 
 def shards(queries, key_rows, value_rows, gate_in, gate_out, kernel_taps, norm_gain, cotangent):
     rows = jax.ShapeDtypeStruct((BLOCK, 1024), BF16)
     vmem = pl.BlockSpec(memory_space=pltpu.VMEM)
+    hbm = pl.BlockSpec(memory_space=pl.ANY)
     tile = (HEAD, HEAD)
     dma = pltpu.SemaphoreType.DMA
     outs = pl.pallas_call(
         kernel,
-        out_shape=[rows] * 6 + [jax.ShapeDtypeStruct((8, 128), F32)] * 2,
-        in_specs=[vmem] * 8,
+        out_shape=[rows] * 6 + [jax.ShapeDtypeStruct((FILT, 128), F32), jax.ShapeDtypeStruct((8, 128), F32)],
+        in_specs=[hbm] * 5 + [vmem] * 2 + [hbm],
         out_specs=[vmem] * 8,
         scratch_shapes=[
             pltpu.VMEM((8, 2, *tile), BF16),
@@ -385,24 +506,43 @@
             pltpu.VMEM((2, 8, 128), F32),
             pltpu.VMEM((8, *tile), BF16),
             pltpu.VMEM((8, *tile), BF16),
-            pltpu.VMEM((4096, HEAD), F32),
-            pltpu.VMEM((4096, HEAD), F32),
-            pltpu.VMEM((32, 2, *tile), BF16),
-            pltpu.VMEM((32, 2, *tile), BF16),
+            pltpu.VMEM((HEAD, 1024), F32),
+            pltpu.VMEM((HEAD, 1024), BF16),
+            pltpu.VMEM((1024, HEAD), BF16),
+            pltpu.VMEM((1, 1024), F32),
+            pltpu.VMEM((2, 2, CHUNK, HEAD), F32),
+            pltpu.VMEM((4, 2, CHUNK, HEAD), BF16),
+            pltpu.VMEM((4, 2, CHUNK, HEAD), BF16),
+            pltpu.VMEM((4, 4, 2, *tile), BF16),
+            pltpu.VMEM((16, 2, *tile), BF16),
             pltpu.VMEM((BLOCK + 8, 1024), F32),
             pltpu.VMEM((2, 8, 128), F32),
             pltpu.VMEM((32, 2, 8, 128), F32),
-            dma((32,)), dma((8,)), dma((8,)), dma((8,)), dma((32,)), dma, dma((8,)), dma((32,)), dma((32,)),
+            pltpu.VMEM((BLOCK, 1024), BF16),
+            pltpu.VMEM((BLOCK, 1024), BF16),
+            pltpu.VMEM((BLOCK, 1024), BF16),
+            pltpu.VMEM((16, CHUNK, CHUNK), BF16),
+            pltpu.VMEM((16, 1, CHUNK), F32),
+            dma((5,)),
+            dma((16,)), dma, dma((4,)), dma((4,)),
+            dma((16,)), dma((8,)), dma((8,)), dma((8,)), dma((32,)), dma, dma((8,)), dma((16,)), dma((32,)),
             dma((2,)),
-            dma, dma, dma, dma, dma, dma, dma, dma, dma, dma((2,)),
+            dma((16,)), dma, dma, dma, dma, dma, dma, dma, dma, dma((2,)),
         ],
-        compiler_params=pltpu.CompilerParams(has_side_effects=True, vmem_limit_bytes=56 * 1024 * 1024),
+        compiler_params=pltpu.CompilerParams(collective_id=0, has_side_effects=True, vmem_limit_bytes=56 * 1024 * 1024),
         name="hyena",
     )(
-        queries, key_rows, value_rows, gate_in, gate_out, kernel_taps, norm_gain.reshape(1, -1), cotangent
+        queries, key_rows, value_rows, gate_in, gate_out, kernel_taps.T, norm_gain.reshape(1, -1), cotangent
     )
-    mixed, gq, gk, gv, ggi, ggo, gf, gg = outs
-    return mixed, gq, gk, gv, ggi, ggo, gf[:FILT].T, gg.reshape(-1)
+    mixed, gq, gk, gv, ggi, ggo, gf, gg = pl.pallas_call(
+        handed_on,
+        out_shape=[jax.ShapeDtypeStruct(o.shape, o.dtype) for o in outs],
+        in_specs=[vmem] * 8,
+        out_specs=[pl.BlockSpec(memory_space=pl.ANY)] * 8,
+        scratch_shapes=[dma((8,))],
+        name="results",
+    )(*outs)
+    return mixed, gq, gk, gv, ggi, ggo, gf.T, gg.reshape(-1)
 
 
 def solution(mesh):

time: 139 us -> 92.1 us (0.66)
  Pallas kernels: 128 us -> 91.2 us
  local copies, waits for them, and re-layouts: 9.88 us -> 0 us
    pallas_call x1 -> x2, Pallas kernels: 128 us -> 91.2 us  [the longest x1 88.7 us: shards(): pl.pallas_call(kernel, out_shape=[rows] * 6 + [jax.ShapeDtypeStruct((FILT...]
    unnamed x22 -> x0, local copies, waits for them, and re-layouts: 9.28 us -> none
where the time goes in v2:
time: 92.1 us; the launch traced here: 91.9 us
  Pallas kernels  91.2 us (99%)
    pallas_call x1, Pallas kernels, shards(): pl.pallas_call(kernel, out_shape=[rows] * 6 + [jax.ShapeDtypeStruct((FILT...  88.7 us
    pallas_call x1, Pallas kernels, shards(): pl.pallas_call(handed_on, out_shape=[jax.ShapeDtypeStruct(o.shape, o.dtyp...  2.56 us

profile of v2, /device:TPU:0, one launch (start us, length us, event | category | flops | bytes accessed | tf_op | source)
XLA Modules:
  0.0 91.9 jit_solution(12191189366065627400)
XLA Ops:
  0.6 88.7 %hyena.1 = (bf16[128,1024]{1,0:T(8,128)(2,1)}, bf16[128,1024]{1,0:T(8,128)(2,1)}, bf16[128,1024]{1,0:T(8,128)(2,1)}, bf16[128,1024]{1,0:T(8,128)(2,1)}, bf16[128...) custom-call(bf16[128,1024]{1,0:T(8,128)(2,1)} %q_any.1, ...), custom_call_target="tpu_custom_call" | custom-call | tf_op jit(solution)/shard_map/hyena/pallas_call | solution.py:486
  89.3 2.6 %results.1 = (bf16[128,1024]{1,0:T(8,128)(2,1)}, bf16[128,1024]{1,0:T(8,128)(2,1)}, bf16[128,1024]{1,0:T(8,128)(2,1)}, bf16[128,1024]{1,0:T(8,128)(2,1)}, bf16[1...) custom-call(bf16[128,1024]{1,0:T(8,128)(2,1)} %get-tuple-element.24.refs_0_, ...), custom_call_target="tpu_custom_call" | custom-call | tf_op jit(solution)/shard_map/results/pallas_call | solution.py:537

commit v3 on v2

--- a/solution.py
+++ b/solution.py
@@ -30,9 +30,9 @@
 def kernel(
     q_any, k_any, v_any, gi_any, go_any, taps_ref, gain_ref, cot_any,
     mixed_ref, gq_ref, gk_ref, gv_ref, ggi_ref, ggo_ref, gf_ref, gg_ref,
-    kvs, qs, ssrc, kvb, qb, sb, du, dz, ot, lse2, osrc, ob, stat_in, tot, hst,
-    dqs, dqb, dq_acc, d_out_t, d_rows, delta, kv_acc, sibs, sibb, dkvs, dkvb, zx, gsrc, gin,
-    gi_ref, go_ref, cot_ref, wbuf, tops, in_sem, relay_send, relay_recv, sib_send, sib_recv,
+    kvs, qs, ssrc, kvb, qb, sb, du, dz, ot, lse2, osrc, ob, sum_sets, sum_heads, tot, hst,
+    dqs, dqb, f_top, f_norm, dq_acc, d_out_t, d_rows, delta, kv_acc, sibs, sibb, dkvs, dkvb, zx, g_near, g_far,
+    gi_ref, go_ref, cot_ref, wbuf, tops, su_send, su_recv, gx_send, gx_recv, in_sem, relay_send, relay_recv, sib_send, sib_recv,
     kv_send, q_send, s_send, o_send, st_send, h_send, dq_send, dkv_send, g_send, rim_send,
     kv_recv, q_recv, s_recv, o_recv, st_recv, h_recv, dq_recv, dkv_recv, g_recv, rim_recv,
 ):
@@ -44,7 +44,6 @@
     hl0, m0 = host // 2, host % 2
     home_chan = zh * 2 + z
     r0 = m0 * 2 + core
-    head0 = home_chan * 8 + hl0
 
     def chip(bit, e):
         return (e // 4) * 8 + bit * 4 + e % 4
@@ -76,38 +75,60 @@
     def arrived(buf, recv_sem):
         pltpu.make_async_copy(buf, buf, recv_sem).wait()
 
+    def moved(i, sign):
+        step = (i * 5) % 16
+        return ((x + sign * (step // 4) + 4) % 4) * 4 + (y + sign * (step % 4) + 4) % 4
+
     def kv_plan(i):
-        e = (host + i) % 16
+        e = moved(i, 1)
         return (
             kvs.at[e // 2], kvb.at[p], kv_send.at[i], kv_recv.at[p // 2],
             chip(core, e), zh * 2 + p % 2,
         )
 
+    def relay_source(i):
+        return chip(i % 2, moved(i - i % 2 + (y + core) % 2, -1))
+
     def relay_plan(i):
-        e = (host - 2 * (i // 2) - (host + core) % 2 + 16) % 16
-        source = chip(i % 2, e)
+        source = relay_source(i)
         return (
             kvb.at[source], kvb.at[source], relay_send.at[i], relay_recv,
             p, zh * 2 + 1 - core, kv_recv.at[source // 2],
         )
 
+    last_chunk = 7 - 2 * m0
+
+    def kv_wanted(i, act):
+        @pl.when(jnp.logical_or(own_chunk <= 5, (i + y) % 2 == 0))
+        def _():
+            act(*kv_plan(i))
+
+    def relay_wanted(i, act):
+        @pl.when(relay_source(i) // 4 <= last_chunk)
+        def _():
+            act(*relay_plan(i))
+
+    def loop(count, act, first=0):
+        lax.fori_loop(first, count, lambda i, _: (act(i), 0)[1], 0)
+
+    own_chunk = p // 4
+
     def relay(block, dst, send_sem, recv_sem, p2, chan2, landed):
         arrived(block, landed)
         send(block, dst, send_sem, recv_sem, p2, chan2)
 
-    own_chunk = p // 4
     own_r = jnp.minimum(own_chunk, 7 - own_chunk)
     own_slot = (own_chunk // 4) * 4 + p % 4
 
     def q_plan(i):
-        hl = (hl0 + i) % 8
+        hl = (hl0 + 3 * i) % 8
         return (
             qs.at[hl], qb.at[own_slot], q_send.at[i], q_recv,
             chip(core, hl * 2 + own_r // 2), zh * 2 + own_r % 2,
         )
 
     def s_plan(i):
-        hl = (hl0 + i) % 8
+        hl = (hl0 + 3 * i) % 8
         return (
             ssrc.at[hl], sb.at[own_slot], s_send.at[i], s_recv,
             chip(core, hl * 2 + own_r // 2), zh * 2 + own_r % 2,
@@ -117,12 +138,12 @@
         return jnp.where(slot < 4, r0 * 4 + slot, (7 - r0) * 4 + slot - 4)
 
     def o_plan(i):
-        return osrc.at[i], ob.at[hl0], o_send.at[i], o_recv, slot_home(i), home_chan
+        slot = ((i + x) % 2) * 4 + (y + i // 2) % 4
+        return osrc.at[slot], ob.at[hl0], o_send.at[i], o_recv, slot_home(slot), home_chan
 
     def dq_plan(i):
-        return dqs.at[i], dqb.at[hl0], dq_send.at[i], dq_recv, slot_home(i), home_chan
-
-    last_chunk = 7 - 2 * m0
+        slot = ((i + x) % 2) * 4 + (y + i // 2) % 4
+        return dqs.at[slot], dqb.at[hl0], dq_send.at[i], dq_recv, slot_home(slot), home_chan
 
     def dkv_plan(i):
         return (
@@ -147,14 +168,25 @@
             sent(*dkv_plan(i))
 
     def st_plan(i):
-        g = (head0 + i) % 32
+        g = (home_chan + i) % 4
         return (
-            stat_in.at[head0], stat_in.at[head0], st_send.at[i], st_recv,
-            chip((g // 8) % 2, (g % 8) * 2 + m0), (g // 16) * 2 + core,
+            sum_sets.at[home_chan], sum_sets.at[home_chan], st_send.at[i], st_recv,
+            chip(g % 2, host), (g // 2) * 2 + core,
+        )
+
+    def su_plan(i):
+        hl = (hl0 + i) % 8
+        return (
+            sum_heads.at[hl0], sum_heads.at[hl0], su_send.at[i], su_recv,
+            chip(z, hl * 2 + m0), chan,
         )
 
     def g_plan(i):
-        return gsrc, gin.at[p], g_send.at[i], g_recv, (p + i) % 32, chan
+        g = (z * 4 + y + i) % 8
+        return g_near.at[z * 4 + y], g_near.at[z * 4 + y], g_send.at[i], g_recv, x * 8 + g, chan
+
+    def gx_plan(i):
+        return g_far.at[x], g_far.at[x], gx_send.at[i], gx_recv, ((x + i) % 4) * 8 + z * 4 + y, chan
 
     def each(plan, count, act, first=0):
         lax.fori_loop(first, count, lambda i, _: (act(*plan(i)), 0)[1], 0)
@@ -170,13 +202,13 @@
 
     def greet_far(i, _):
         pl.semaphore_signal(
-            barrier, inc=1, device_id={"ctx": i * 2 + m0, "chan": (1 - zh) * 2 + core},
+            barrier, inc=1, device_id={"ctx": chip(i, host), "chan": (1 - zh) * 2 + core},
             device_id_type=pl.DeviceIdType.MESH,
         )
         return 0
 
     lax.fori_loop(1, 64, greet, 0)
-    lax.fori_loop(0, 16, greet_far, 0)
+    lax.fori_loop(0, 2, greet_far, 0)
     wide_in = [
         pltpu.make_async_copy(src, dst, in_sem.at[j])
         for j, (src, dst) in enumerate(((cot_any, cot_ref), (go_any, go_ref), (gi_any, gi_ref)))
@@ -209,14 +241,14 @@
     pltpu.make_async_copy(kvs, kvs, in_sem.at[3]).wait()
     pltpu.make_async_copy(qs, qs, in_sem.at[4]).wait()
     wide_in[2].wait()
-    pl.semaphore_wait(barrier, 79)
+    pl.semaphore_wait(barrier, 65)
 
     @pl.when(p > 0)
     def _():
         du_rim.start()
 
-    each(kv_plan, 16, send)
     each(q_plan, 8, send)
+    loop(16, lambda i: kv_wanted(i, send))
 
     @pl.when(p == 31)
     def _():
@@ -234,10 +266,6 @@
         dz[:, cols] = total
         ssrc[hl] = (total * gi_ref[:, cols].astype(F32) * gain[:, cols]).astype(BF16)
 
-    each(relay_plan, 16, relay)
-    each(s_plan, 8, send)
-    arrived(kvb.at[pl.ds(0, 16)], relay_recv)
-    arrived(qb, q_recv)
     below = lax.broadcasted_iota(jnp.int32, (CHUNK, CHUNK), 0) <= lax.broadcasted_iota(
         jnp.int32, (CHUNK, CHUNK), 1
     )
@@ -248,53 +276,82 @@
     def values_of(kt):
         return kvb[pl.ds(kt * 4, 4), 1].reshape(CHUNK, HEAD)
 
-    s_waited = False
+    chunks = (r0, 7 - r0)
+    f_top[...] = jnp.full((1, 1024), NEG, F32)
+    f_norm[...] = jnp.zeros((1, 1024), F32)
+    ot[...] = jnp.zeros((HEAD, 1024), F32)
+
+    def forward(qc, kt, masked):
+        rows = slice(qc * CHUNK, (qc + 1) * CHUNK)
+        s = dot(keys_of(kt), qb[pl.ds(qc * 4, 4)].reshape(CHUNK, HEAD), 1, 1)
+        if masked:
+            s = jnp.where(below, s, NEG)
+        top = f_top[:, rows]
+        new_top = jnp.maximum(top, jnp.max(s, axis=0, keepdims=True))
+        w = jnp.exp2(s * SCALE2 - new_top * SCALE2)
+        w_low = w.astype(BF16)
+        wbuf[qc * 8 + kt] = w_low
+        tops[qc * 8 + kt] = new_top
+        fade = jnp.exp2((top - new_top) * SCALE2)
+        f_top[:, rows] = new_top
+        f_norm[:, rows] = f_norm[:, rows] * fade + jnp.sum(w, axis=0, keepdims=True)
+        ot[:, rows] = ot[:, rows] * fade + dot(values_of(kt), w_low, 0, 0)
+
+    def forward_chunk(kt, _):
+        for qc in range(2):
+
+            @pl.when(kt < chunks[qc])
+            def _():
+                forward(qc, kt, False)
+
+            @pl.when(kt == chunks[qc])
+            def _():
+                forward(qc, kt, True)
+
+        return 0
+
+    loop(16, lambda i: relay_wanted(i, relay))
+    each(s_plan, 8, send)
+
+    @pl.when(m0 == 0)
+    def _():
+        arrived(kvb.at[pl.ds(0, 16)], relay_recv)
+
+    @pl.when(m0 == 1)
+    def _():
+        arrived(kvb.at[pl.ds(0, 12)], relay_recv)
+
+    arrived(qb, q_recv)
+    lax.fori_loop(0, 8, forward_chunk, 0)
+    arrived(sb, s_recv)
     for qc in range(2):
-        chunk = r0 if qc == 0 else 7 - r0
         rows = slice(qc * CHUNK, (qc + 1) * CHUNK)
-        q_rows = qb[pl.ds(qc * 4, 4)].reshape(CHUNK, HEAD)
-
-        def forward(kt, carry, masked, q_rows=q_rows, qc=qc):
-            top, norm, acc = carry
-            s = dot(keys_of(kt), q_rows, 1, 1)
-            if masked:
-                s = jnp.where(below, s, NEG)
-            new_top = jnp.maximum(top, jnp.max(s, axis=0, keepdims=True))
-            w = jnp.exp2(s * SCALE2 - new_top * SCALE2)
-            w_low = w.astype(BF16)
-            wbuf[qc * 8 + kt] = w_low
-            tops[qc * 8 + kt] = new_top
-            fade = jnp.exp2((top - new_top) * SCALE2)
-            norm = norm * fade + jnp.sum(w, axis=0, keepdims=True)
-            acc = acc * fade + dot(values_of(kt), w_low, 0, 0)
-            return new_top, norm, acc
-
-        carry = (
-            jnp.full((1, CHUNK), NEG, F32), jnp.zeros((1, CHUNK), F32), jnp.zeros((HEAD, CHUNK), F32)
-        )
-        carry = lax.fori_loop(0, chunk, lambda kt, c: forward(kt, c, False), carry)
-        top, norm, acc = forward(chunk, carry, True)
-        out = (acc * (1.0 / norm)).astype(BF16)
+        norm = f_norm[:, rows]
+        out = (ot[:, rows] * (1.0 / norm)).astype(BF16)
         out_wide = out.astype(F32)
         ot[:, rows] = out_wide
-        lse2[:, rows] = top * SCALE2 + jnp.log2(norm)
+        lse2[:, rows] = f_top[:, rows] * SCALE2 + jnp.log2(norm)
         osrc[pl.ds(qc * 4, 4)] = out_wide.T.astype(BF16).reshape(4, HEAD, HEAD)
-        if not s_waited:
-            arrived(sb, s_recv)
-            s_waited = True
         s_t = sb[pl.ds(qc * 4, 4)].reshape(CHUNK, HEAD).astype(F32).T
         squares = jnp.sum(out_wide * out_wide, axis=0, keepdims=True)
         dots = jnp.sum(s_t * out_wide, axis=0, keepdims=True)
         for j in range(4):
             at = slice(j * HEAD, (j + 1) * HEAD)
-            stat_in[head0, 0, qc * 4 + j : qc * 4 + j + 1, :] = squares[:, at]
-            stat_in[head0, 1, qc * 4 + j : qc * 4 + j + 1, :] = dots[:, at]
-
-    each(st_plan, 32, send, 1)
+            sum_sets[home_chan, 0, qc * 4 + j : qc * 4 + j + 1, :] = squares[:, at]
+            sum_sets[home_chan, 1, qc * 4 + j : qc * 4 + j + 1, :] = dots[:, at]
+
+    each(st_plan, 4, send, 1)
     each(o_plan, 8, send)
-    arrived(stat_in.at[pl.ds(0, 31)], st_recv)
-    tot[...] = jnp.sum(stat_in[...], axis=0)
-
+    loop(16, lambda i: kv_wanted(i, sent))
+    each(q_plan, 8, sent)
+    loop(16, lambda i: relay_wanted(i, lambda *a: sent(*a[:6])))
+    arrived(sum_sets.at[pl.ds(0, 3)], st_recv)
+    sum_heads[hl0] = jnp.sum(sum_sets[...], axis=0)
+    each(su_plan, 8, send, 1)
+    each(st_plan, 4, sent, 1)
+    each(s_plan, 8, sent)
+    arrived(sum_heads.at[pl.ds(0, 7)], su_recv)
+    tot[...] = jnp.sum(sum_heads[...], axis=0)
     home_slot = jnp.where(r0 % 2 == hl0 // 4, hl0 % 4, 4 + hl0 % 4)
     h_args = (tot, hst, h_send, h_recv, slot_home(home_slot), home_chan)
     send(*h_args)
@@ -341,15 +398,14 @@
             for which, scale in ((0, SCALE), (1, 1.0)):
                 both = kv_acc[slot, which] * scale + sibb[kt // 2, which].astype(F32)
                 dkvs[kt // 2, :, which] = both.astype(BF16).reshape(4, HEAD, HEAD)
-            for j in range(4):
-                send(*dkv_plan((kt // 2) * 4 + j))
+            loop((kt // 2) * 4 + 4, lambda i: send(*dkv_plan(i)), (kt // 2) * 4)
+
+    first = hl0 + 2 * y
 
     def key_chunk(t, _):
-        kt, slot = (hl0 + t) % 8, t % 2
+        kt, slot = (first + t) % 8, t % 2
         for qc in (1, 0):
-            chunk = r0 if qc == 0 else 7 - r0
-
-            @pl.when(kt <= chunk)
+            @pl.when(kt <= chunks[qc])
             def _():
                 backward(qc, kt, slot)
 
@@ -369,13 +425,7 @@
 
         return 0
 
-    lax.fori_loop(0, 8, key_chunk, 0)
-    finish((hl0 + 7) % 8, 1)
-    for qc in range(2):
-        dq = dq_acc[:, qc * CHUNK : (qc + 1) * CHUNK] * SCALE
-        dqs[pl.ds(qc * 4, 4)] = dq.T.astype(BF16).reshape(4, HEAD, HEAD)
-    each(dq_plan, 8, send)
-
+    lax.fori_loop(0, 4, key_chunk, 0)
     arrived(ob, o_recv)
     arrived(hst, h_recv)
     square_row = hst[0, pl.ds(own_slot, 1), :]
@@ -388,7 +438,7 @@
         gate = gi_ref[:, cols].astype(F32)
         zx[pl.ds(8, BLOCK), cols] = gate * normed
         ggi_ref[:, cols] = (dz[:, cols] * normed).astype(BF16)
-        gsrc[1, hl : hl + 1, :] = jnp.sum(dz[:, cols] * gate * a_hat, axis=0, keepdims=True)
+        g_near[z * 4 + y, 1, hl : hl + 1, :] = jnp.sum(dz[:, cols] * gate * a_hat, axis=0, keepdims=True)
 
     @pl.when(p < 31)
     def _():
@@ -398,6 +448,7 @@
     def _():
         zx[pl.ds(0, 8), :] = jnp.zeros((8, 1024), F32)
 
+    lax.fori_loop(4, 6, key_chunk, 0)
     @pl.when(p > 0)
     def _():
         z_rim.wait_recv()
@@ -416,14 +467,38 @@
         tap_sums.append(jnp.concatenate(sums, axis=0))
         mixed_ref[:, cols] = (go_ref[:, cols].astype(F32) * conv).astype(BF16)
         ggo_ref[:, cols] = (cot_ref[:, cols].astype(F32) * conv).astype(BF16)
-    gsrc[0] = dot(jnp.concatenate(tap_sums, axis=1), spread, 1, 1, lax.Precision.HIGHEST)
-    each(g_plan, 32, send, 1)
-
-    arrived(gin.at[pl.ds(0, 31)], g_recv)
-    gin[p] = gsrc[...]
-    g_total = jnp.sum(gin[...], axis=0)
+    g_near[z * 4 + y, 0] = dot(jnp.concatenate(tap_sums, axis=1), spread, 1, 1, lax.Precision.HIGHEST)
+    each(g_plan, 8, send, 1)
+    lax.fori_loop(6, 8, key_chunk, 0)
+    finish((first + 7) % 8, 1)
+    for qc in range(2):
+        dq = dq_acc[:, qc * CHUNK : (qc + 1) * CHUNK] * SCALE
+        dqs[pl.ds(qc * 4, 4)] = dq.T.astype(BF16).reshape(4, HEAD, HEAD)
+    each(dq_plan, 8, send)
+    arrived(g_near.at[pl.ds(0, 7)], g_recv)
+    g_far[x] = jnp.sum(g_near[...], axis=0)
+    each(gx_plan, 4, send, 1)
+    each(o_plan, 8, sent)
+    sent(*h_args)
+    each(su_plan, 8, sent, 1)
+    each(g_plan, 8, sent, 1)
+    arrived(g_far.at[pl.ds(0, 3)], gx_recv)
+    g_total = jnp.sum(g_far[...], axis=0)
     gf_ref[...] = g_total[0, :FILT]
     gg_ref[...] = g_total[1]
+    lax.fori_loop(0, 4, lambda i, _: (sib_sent(i), 0)[1], 0)
+    lax.fori_loop(0, 16, lambda i, _: (dkv_sent(i), 0)[1], 0)
+    each(dq_plan, 8, sent)
+    each(gx_plan, 4, sent, 1)
+
+    @pl.when(p > 0)
+    def _():
+        du_rim.wait_send()
+
+    @pl.when(p < 31)
+    def _():
+        z_rim.wait_send()
+
     arrived(dqb, dq_recv)
 
     def all_keys(parts):
@@ -447,34 +522,18 @@
     def _():
         all_keys(1)
 
-    each(kv_plan, 16, sent)
-    each(relay_plan, 16, lambda *a: sent(*a[:6]))
-    lax.fori_loop(0, 4, lambda i, _: (sib_sent(i), 0)[1], 0)
-    each(q_plan, 8, sent)
-    each(s_plan, 8, sent)
-    each(st_plan, 32, sent, 1)
-    each(o_plan, 8, sent)
-    sent(*h_args)
-    lax.fori_loop(0, 16, lambda i, _: (dkv_sent(i), 0)[1], 0)
-    each(dq_plan, 8, sent)
-    each(g_plan, 32, sent, 1)
-
-    @pl.when(p > 0)
-    def _():
-        du_rim.wait_send()
-
-    @pl.when(p < 31)
-    def _():
-        z_rim.wait_send()
-
 
 def handed_on(*refs):
-    sems = refs[16]
-    copies = [pltpu.make_async_copy(refs[i], refs[8 + i], sems.at[i]) for i in range(8)]
-    for copy in copies:
-        copy.start()
-    for copy in copies:
-        copy.wait()
+    held, in_sem, out_sem = refs[16:24], refs[24], refs[25]
+    loads = [pltpu.make_async_copy(refs[i], held[i], in_sem.at[i]) for i in range(8)]
+    stores = [pltpu.make_async_copy(held[i], refs[8 + i], out_sem.at[i]) for i in range(8)]
+    for load in loads:
+        load.start()
+    for load, store in zip(loads, stores):
+        load.wait()
+        store.start()
+    for store in stores:
+        store.wait()
 
 
 def shards(queries, key_rows, value_rows, gate_in, gate_out, kernel_taps, norm_gain, cotangent):
@@ -501,11 +560,14 @@
             pltpu.VMEM((1, 1024), F32),
             pltpu.VMEM((8, *tile), BF16),
             pltpu.VMEM((8, *tile), BF16),
-            pltpu.VMEM((32, 2, 8, 128), F32),
+            pltpu.VMEM((4, 2, 8, 128), F32),
+            pltpu.VMEM((8, 2, 8, 128), F32),
             pltpu.VMEM((2, 8, 128), F32),
             pltpu.VMEM((2, 8, 128), F32),
             pltpu.VMEM((8, *tile), BF16),
             pltpu.VMEM((8, *tile), BF16),
+            pltpu.VMEM((1, 1024), F32),
+            pltpu.VMEM((1, 1024), F32),
             pltpu.VMEM((HEAD, 1024), F32),
             pltpu.VMEM((HEAD, 1024), BF16),
             pltpu.VMEM((1024, HEAD), BF16),
@@ -516,16 +578,17 @@
             pltpu.VMEM((4, 4, 2, *tile), BF16),
             pltpu.VMEM((16, 2, *tile), BF16),
             pltpu.VMEM((BLOCK + 8, 1024), F32),
-            pltpu.VMEM((2, 8, 128), F32),
-            pltpu.VMEM((32, 2, 8, 128), F32),
+            pltpu.VMEM((8, 2, 8, 128), F32),
+            pltpu.VMEM((4, 2, 8, 128), F32),
             pltpu.VMEM((BLOCK, 1024), BF16),
             pltpu.VMEM((BLOCK, 1024), BF16),
             pltpu.VMEM((BLOCK, 1024), BF16),
             pltpu.VMEM((16, CHUNK, CHUNK), BF16),
             pltpu.VMEM((16, 1, CHUNK), F32),
+            dma((8,)), dma, dma((4,)), dma,
             dma((5,)),
             dma((16,)), dma, dma((4,)), dma((4,)),
-            dma((16,)), dma((8,)), dma((8,)), dma((8,)), dma((32,)), dma, dma((8,)), dma((16,)), dma((32,)),
+            dma((16,)), dma((8,)), dma((8,)), dma((8,)), dma((4,)), dma, dma((8,)), dma((16,)), dma((8,)),
             dma((2,)),
             dma((16,)), dma, dma, dma, dma, dma, dma, dma, dma, dma((2,)),
         ],
@@ -537,9 +600,9 @@
     mixed, gq, gk, gv, ggi, ggo, gf, gg = pl.pallas_call(
         handed_on,
         out_shape=[jax.ShapeDtypeStruct(o.shape, o.dtype) for o in outs],
-        in_specs=[vmem] * 8,
-        out_specs=[pl.BlockSpec(memory_space=pl.ANY)] * 8,
-        scratch_shapes=[dma((8,))],
+        in_specs=[hbm] * 8,
+        out_specs=[hbm] * 8,
+        scratch_shapes=[pltpu.VMEM(o.shape, o.dtype) for o in outs] + [dma((8,)), dma((8,))],
         name="results",
     )(*outs)
     return mixed, gq, gk, gv, ggi, ggo, gf.T, gg.reshape(-1)

time: 92.1 us -> 83.3 us (0.904)
  the two profiles are of different devices: /device:TPU:0 before, /device:TPU:31 now
where the time goes in v3:
time: 83.3 us; the launch traced here: 83.1 us
  Pallas kernels  82.5 us (99%)
    pallas_call x1, Pallas kernels, shards(): pl.pallas_call(kernel, out_shape=[rows] * 6 + [jax.ShapeDtypeStruct((FILT...  80.2 us
    pallas_call x1, Pallas kernels, shards(): pl.pallas_call(handed_on, out_shape=[jax.ShapeDtypeStruct(o.shape, o.dtyp...  2.23 us

profile of v3, /device:TPU:31, one launch (start us, length us, event | category | flops | bytes accessed | tf_op | source)
XLA Modules:
  0.0 83.1 jit_solution(9323653717606607594)
XLA Ops:
  0.6 80.2 %hyena.1 = (bf16[128,1024]{1,0:T(8,128)(2,1)}, bf16[128,1024]{1,0:T(8,128)(2,1)}, bf16[128,1024]{1,0:T(8,128)(2,1)}, bf16[128,1024]{1,0:T(8,128)(2,1)}, bf16[128...) custom-call(bf16[128,1024]{1,0:T(8,128)(2,1)} %q_any.1, ...), custom_call_target="tpu_custom_call" | custom-call | tf_op jit(solution)/shard_map/hyena/pallas_call | solution.py:545
  80.9 2.2 %results.1 = (bf16[128,1024]{1,0:T(8,128)(2,1)}, bf16[128,1024]{1,0:T(8,128)(2,1)}, bf16[128,1024]{1,0:T(8,128)(2,1)}, bf16[128,1024]{1,0:T(8,128)(2,1)}, bf16[1...) custom-call(bf16[128,1024]{1,0:T(8,128)(2,1)} %get-tuple-element.24.refs_0_, ...), custom_call_target="tpu_custom_call" | custom-call | tf_op jit(solution)/shard_map/results/pallas_call | solution.py:600

commit v4 on v3

--- a/solution.py
+++ b/solution.py
@@ -40,13 +40,16 @@
     chan = lax.axis_index("chan")
     zh, core = chan // 2, chan % 2
     x, z, y = p // 8, (p // 4) % 2, p % 4
-    host = x * 4 + y
-    hl0, m0 = host // 2, host % 2
+    hl0, m0 = x * 2 + y // 2, (x + y) % 2
+    host = hl0 * 2 + m0
     home_chan = zh * 2 + z
     r0 = m0 * 2 + core
 
+    def place(bit, e):
+        return (e // 4) * 8 + bit * 4 + e % 4
+
     def chip(bit, e):
-        return (e // 4) * 8 + bit * 4 + e % 4
+        return (e // 4) * 8 + bit * 4 + ((e // 2) % 2) * 2 + (e % 2 + e // 4) % 2
 
     def send(src, dst, send_sem, recv_sem, p2, chan2):
         own = jnp.logical_and(p2 == p, chan2 == chan)
@@ -83,11 +86,11 @@
         e = moved(i, 1)
         return (
             kvs.at[e // 2], kvb.at[p], kv_send.at[i], kv_recv.at[p // 2],
-            chip(core, e), zh * 2 + p % 2,
+            place(core, e), zh * 2 + p % 2,
         )
 
     def relay_source(i):
-        return chip(i % 2, moved(i - i % 2 + (y + core) % 2, -1))
+        return place(i % 2, moved(i - i % 2 + (y + core) % 2, -1))
 
     def relay_plan(i):
         source = relay_source(i)
@@ -99,7 +102,7 @@
     last_chunk = 7 - 2 * m0
 
     def kv_wanted(i, act):
-        @pl.when(jnp.logical_or(own_chunk <= 5, (i + y) % 2 == 0))
+        @pl.when(jnp.logical_or(own_chunk <= 5, ((i * 5 // 4) + i + x + y) % 2 == 0))
         def _():
             act(*kv_plan(i))
 
@@ -341,15 +344,10 @@
             sum_sets[home_chan, 1, qc * 4 + j : qc * 4 + j + 1, :] = dots[:, at]
 
     each(st_plan, 4, send, 1)
-    each(o_plan, 8, send)
-    loop(16, lambda i: kv_wanted(i, sent))
-    each(q_plan, 8, sent)
-    loop(16, lambda i: relay_wanted(i, lambda *a: sent(*a[:6])))
     arrived(sum_sets.at[pl.ds(0, 3)], st_recv)
     sum_heads[hl0] = jnp.sum(sum_sets[...], axis=0)
     each(su_plan, 8, send, 1)
-    each(st_plan, 4, sent, 1)
-    each(s_plan, 8, sent)
+    each(o_plan, 8, send)
     arrived(sum_heads.at[pl.ds(0, 7)], su_recv)
     tot[...] = jnp.sum(sum_heads[...], axis=0)
     home_slot = jnp.where(r0 % 2 == hl0 // 4, hl0 % 4, 4 + hl0 % 4)
@@ -486,6 +484,11 @@
     g_total = jnp.sum(g_far[...], axis=0)
     gf_ref[...] = g_total[0, :FILT]
     gg_ref[...] = g_total[1]
+    loop(16, lambda i: kv_wanted(i, sent))
+    each(q_plan, 8, sent)
+    loop(16, lambda i: relay_wanted(i, lambda *a: sent(*a[:6])))
+    each(st_plan, 4, sent, 1)
+    each(s_plan, 8, sent)
     lax.fori_loop(0, 4, lambda i, _: (sib_sent(i), 0)[1], 0)
     lax.fori_loop(0, 16, lambda i, _: (dkv_sent(i), 0)[1], 0)
     each(dq_plan, 8, sent)

time: 83.3 us -> 80.2 us (0.963)
  the two profiles are of different devices: /device:TPU:31 before, /device:TPU:0 now
where the time goes in v4:
time: 80.2 us; the launch traced here: 79.3 us
  Pallas kernels  78.6 us (98%)
    pallas_call x1, Pallas kernels, shards(): pl.pallas_call(kernel, out_shape=[rows] * 6 + [jax.ShapeDtypeStruct((FILT...  76.4 us
    pallas_call x1, Pallas kernels, shards(): pl.pallas_call(handed_on, out_shape=[jax.ShapeDtypeStruct(o.shape, o.dtyp...  2.23 us

profile of v4, /device:TPU:0, one launch (start us, length us, event | category | flops | bytes accessed | tf_op | source)
XLA Modules:
  0.0 79.3 jit_solution(571674809795040577)
XLA Ops:
  0.6 76.4 %hyena.1 = (bf16[128,1024]{1,0:T(8,128)(2,1)}, bf16[128,1024]{1,0:T(8,128)(2,1)}, bf16[128,1024]{1,0:T(8,128)(2,1)}, bf16[128,1024]{1,0:T(8,128)(2,1)}, bf16[128...) custom-call(bf16[128,1024]{1,0:T(8,128)(2,1)} %q_any.1, ...), custom_call_target="tpu_custom_call" | custom-call | tf_op jit(solution)/shard_map/hyena/pallas_call | solution.py:548
  77.0 2.2 %results.1 = (bf16[128,1024]{1,0:T(8,128)(2,1)}, bf16[128,1024]{1,0:T(8,128)(2,1)}, bf16[128,1024]{1,0:T(8,128)(2,1)}, bf16[128,1024]{1,0:T(8,128)(2,1)}, bf16[1...) custom-call(bf16[128,1024]{1,0:T(8,128)(2,1)} %get-tuple-element.24.refs_0_, ...), custom_call_target="tpu_custom_call" | custom-call | tf_op jit(solution)/shard_map/results/pallas_call | solution.py:603

commit v5 on v4

--- a/solution.py
+++ b/solution.py
@@ -31,7 +31,7 @@
     q_any, k_any, v_any, gi_any, go_any, taps_ref, gain_ref, cot_any,
     mixed_ref, gq_ref, gk_ref, gv_ref, ggi_ref, ggo_ref, gf_ref, gg_ref,
     kvs, qs, ssrc, kvb, qb, sb, du, dz, ot, lse2, osrc, ob, sum_sets, sum_heads, tot, hst,
-    dqs, dqb, f_top, f_norm, dq_acc, d_out_t, d_rows, delta, kv_acc, sibs, sibb, dkvs, dkvb, zx, g_near, g_far,
+    dqs, dqb, f_top, f_norm, s_keep, dq_acc, d_out_t, d_rows, delta, kv_acc, sibs, sibb, dkvs, dkvb, zx, g_near, g_far,
     gi_ref, go_ref, cot_ref, wbuf, tops, su_send, su_recv, gx_send, gx_recv, in_sem, relay_send, relay_recv, sib_send, sib_recv,
     kv_send, q_send, s_send, o_send, st_send, h_send, dq_send, dkv_send, g_send, rim_send,
     kv_recv, q_recv, s_recv, o_recv, st_recv, h_recv, dq_recv, dkv_recv, g_recv, rim_recv,
@@ -334,8 +334,8 @@
         out_wide = out.astype(F32)
         ot[:, rows] = out_wide
         lse2[:, rows] = f_top[:, rows] * SCALE2 + jnp.log2(norm)
-        osrc[pl.ds(qc * 4, 4)] = out_wide.T.astype(BF16).reshape(4, HEAD, HEAD)
         s_t = sb[pl.ds(qc * 4, 4)].reshape(CHUNK, HEAD).astype(F32).T
+        s_keep[:, rows] = s_t
         squares = jnp.sum(out_wide * out_wide, axis=0, keepdims=True)
         dots = jnp.sum(s_t * out_wide, axis=0, keepdims=True)
         for j in range(4):
@@ -344,6 +344,9 @@
             sum_sets[home_chan, 1, qc * 4 + j : qc * 4 + j + 1, :] = dots[:, at]
 
     each(st_plan, 4, send, 1)
+    for qc in range(2):
+        out_wide = ot[:, qc * CHUNK : (qc + 1) * CHUNK]
+        osrc[pl.ds(qc * 4, 4)] = out_wide.T.astype(BF16).reshape(4, HEAD, HEAD)
     arrived(sum_sets.at[pl.ds(0, 3)], st_recv)
     sum_heads[hl0] = jnp.sum(sum_sets[...], axis=0)
     each(su_plan, 8, send, 1)
@@ -359,7 +362,7 @@
 
     for qc in range(2):
         rows = slice(qc * CHUNK, (qc + 1) * CHUNK)
-        s_t = sb[pl.ds(qc * 4, 4)].reshape(CHUNK, HEAD).astype(F32).T
+        s_t = s_keep[:, rows]
         out_wide = ot[:, rows]
 
         def lanes(a, qc=qc):
@@ -572,6 +575,7 @@
             pltpu.VMEM((1, 1024), F32),
             pltpu.VMEM((1, 1024), F32),
             pltpu.VMEM((HEAD, 1024), F32),
+            pltpu.VMEM((HEAD, 1024), F32),
             pltpu.VMEM((HEAD, 1024), BF16),
             pltpu.VMEM((1024, HEAD), BF16),
             pltpu.VMEM((1, 1024), F32),

time: 80.2 us -> 80.1 us (level)
  no operation moved by 1% of the time
where the time goes in v5:
time: 80.1 us; the launch traced here: 79.2 us
  Pallas kernels  78.6 us (98%)
    pallas_call x1, Pallas kernels, shards(): pl.pallas_call(kernel, out_shape=[rows] * 6 + [jax.ShapeDtypeStruct((FILT...  76.3 us
    pallas_call x1, Pallas kernels, shards(): pl.pallas_call(handed_on, out_shape=[jax.ShapeDtypeStruct(o.shape, o.dtyp...  2.23 us

profile of v5, /device:TPU:0, one launch (start us, length us, event | category | flops | bytes accessed | tf_op | source)
XLA Modules:
  0.0 79.2 jit_solution(5901976656413592942)
XLA Ops:
  0.6 76.3 %hyena.1 = (bf16[128,1024]{1,0:T(8,128)(2,1)}, bf16[128,1024]{1,0:T(8,128)(2,1)}, bf16[128,1024]{1,0:T(8,128)(2,1)}, bf16[128,1024]{1,0:T(8,128)(2,1)}, bf16[128...) custom-call(bf16[128,1024]{1,0:T(8,128)(2,1)} %q_any.1, ...), custom_call_target="tpu_custom_call" | custom-call | tf_op jit(solution)/shard_map/hyena/pallas_call | solution.py:551
  77.0 2.2 %results.1 = (bf16[128,1024]{1,0:T(8,128)(2,1)}, bf16[128,1024]{1,0:T(8,128)(2,1)}, bf16[128,1024]{1,0:T(8,128)(2,1)}, bf16[128,1024]{1,0:T(8,128)(2,1)}, bf16[1...) custom-call(bf16[128,1024]{1,0:T(8,128)(2,1)} %get-tuple-element.24.refs_0_, ...), custom_call_target="tpu_custom_call" | custom-call | tf_op jit(solution)/shard_map/results/pallas_call | solution.py:607
